TPU v7x, 512 devices: a whole 4x4x16 slice. The times are simulated.
512 devices in a mesh: seq: 32 (over z, x_hi), tp: 16 (over y, x_lo, core).
Axes of the slice: x: 4 (x_hi: 2, x_lo: 2; x = x_hi * 2 + x_lo), y: 4, z: 16, core: 2. Of those that a mesh axis runs over, the one named last changes fastest.
Arguments:
- stream_q: bfloat16 [4096, 16384], P('tp', 'seq'), may hold values from -6 to 6
- stream_k: bfloat16 [4096, 16384], P('tp', 'seq'), may hold values from -6 to 6
- stream_v: bfloat16 [4096, 16384], P('tp', 'seq'), may hold values from -6 to 6
- short_taps: float32 [3, 4096, 3], P(None, 'tp'), may hold values from -3 to 3
- filters: float32 [256, 16384], P('tp', 'seq'), may hold values from -2.5 to 2.5
- live_mask: int32 [4096], P('tp'), may hold values from 0 to 1, as said below
- skip_gain: float32 [4096], P('tp'), may hold values from 0.5 to 1.5
Outputs:
- gated_out: bfloat16 [4096, 16384], P('tp', 'seq')
Inputs may be any that keep to these rules, and one draw needn't show every extreme that they name: `live_mask`: in each block of 256 channels the dummy channels, if any, form the block's tail.
All inputs are finite; a program needn't handle non-finite values.
Results may differ from a plain program's by a relative error of at most 0.0054.
Values may be sent and summed in bfloat16 or wider, within the bound.
No kernel may reach another device: no remote copies, remote signals or barrier semaphores. Data moves between devices by JAX's collectives and lax.ppermute only.
A program may use at most 64 MiB of HBM per device.

v0:
```python
import jax
import jax.numpy as jnp
from jax import lax
from jax.sharding import PartitionSpec as P

precise = lax.Precision.HIGH


def factor_sizes(length):
    padded = 2 * length
    inner_size = 1
    while inner_size * 2 * (inner_size * 2) <= padded and length % (inner_size * 2) == 0:
        inner_size = inner_size * 2
    return (inner_size, padded // inner_size)


def angle_table(row_count, col_count, modulus):
    products = (
        jnp.arange(row_count, dtype=jnp.int32)[:, None]
        * jnp.arange(col_count, dtype=jnp.int32)[None, :]
        % modulus
    )
    angles = products.astype(jnp.float32) * (2.0 * jnp.pi / modulus)
    return (jnp.cos(angles), jnp.sin(angles))


def contract(form, left, right):
    return jnp.einsum(form, left, right, precision=precise)


def forward_real(signal, inner_size, outer_size):
    half_size = outer_size // 2
    shaped = signal.reshape(signal.shape[0], half_size, inner_size)
    cosine, sine_table = angle_table(outer_size, half_size, outer_size)
    first_re = contract("kb,rba->rka", cosine, shaped)
    first_im = -contract("kb,rba->rka", sine_table, shaped)
    turn_cos, turn_sin = angle_table(outer_size, inner_size, outer_size * inner_size)
    rot_re = first_re * turn_cos + first_im * turn_sin
    rot_im = first_im * turn_cos - first_re * turn_sin
    small_cos, small_sin = angle_table(inner_size, inner_size, inner_size)
    spec_re = contract("rka,aj->rkj", rot_re, small_cos) + contract(
        "rka,aj->rkj", rot_im, small_sin
    )
    spec_im = contract("rka,aj->rkj", rot_im, small_cos) - contract(
        "rka,aj->rkj", rot_re, small_sin
    )
    return (spec_re, spec_im)


def inverse_real(spec_re, spec_im, inner_size, outer_size):
    half_size = outer_size // 2
    small_cos, small_sin = angle_table(inner_size, inner_size, inner_size)
    back_re = contract("rkj,ja->rka", spec_re, small_cos) - contract(
        "rkj,ja->rka", spec_im, small_sin
    )
    back_im = contract("rkj,ja->rka", spec_im, small_cos) + contract(
        "rkj,ja->rka", spec_re, small_sin
    )
    turn_cos, turn_sin = angle_table(outer_size, inner_size, outer_size * inner_size)
    rot_re = back_re * turn_cos - back_im * turn_sin
    rot_im = back_im * turn_cos + back_re * turn_sin
    cosine, sine_table = angle_table(half_size, outer_size, outer_size)
    signal = contract("bk,rka->rba", cosine, rot_re) - contract("bk,rka->rba", sine_table, rot_im)
    return signal.reshape(signal.shape[0], half_size * inner_size) / (outer_size * inner_size)


def causal_conv(widened, filter_full):
    inner_size, outer_size = factor_sizes(widened.shape[1])
    data_re, data_im = forward_real(widened, inner_size, outer_size)
    kernel_re, kernel_im = forward_real(filter_full, inner_size, outer_size)
    joint_re = data_re * kernel_re - data_im * kernel_im
    joint_im = data_re * kernel_im + data_im * kernel_re
    return inverse_real(joint_re, joint_im, inner_size, outer_size)


def featurize(signal, weights, earlier):
    joined = jnp.concatenate((earlier, signal), axis=1).astype(jnp.float32)
    return (
        weights[:, 0:1] * joined[:, 2:]
        + weights[:, 1:2] * joined[:, 1:-1]
        + weights[:, 2:3] * joined[:, :-2]
    )


def shards(stream_q, stream_k, stream_v, short_taps, filters, live_mask, skip_gain):
    per_group = stream_q.shape[0] // filters.shape[0]
    channel_rows = jnp.repeat(filters, per_group, axis=0)
    filter_full = lax.all_to_all(channel_rows, "seq", split_axis=0, concat_axis=1, tiled=True)
    query_full, key_full, value_full = (
        lax.all_to_all(stream_q, "seq", split_axis=0, concat_axis=1, tiled=True),
        lax.all_to_all(stream_k, "seq", split_axis=0, concat_axis=1, tiled=True),
        lax.all_to_all(stream_v, "seq", split_axis=0, concat_axis=1, tiled=True),
    )
    per_device = query_full.shape[0]
    offset = lax.axis_index("seq") * per_device
    weights = lax.dynamic_slice_in_dim(short_taps, offset, per_device, 1)
    alive_rows = lax.dynamic_slice_in_dim(live_mask, offset, per_device, 0)
    gain_rows = lax.dynamic_slice_in_dim(skip_gain, offset, per_device, 0)
    earlier = jnp.zeros((per_device, 2), jnp.bfloat16)
    feat_query = featurize(query_full, weights[0], earlier)
    feat_key = featurize(key_full, weights[1], earlier)
    feat_value = featurize(value_full, weights[2], earlier)
    product = (feat_key * feat_value).astype(jnp.bfloat16)
    widened = lax.optimization_barrier(product).astype(jnp.float32)
    convolved = causal_conv(widened, filter_full).astype(jnp.bfloat16)
    conv_wide = lax.optimization_barrier(convolved).astype(jnp.float32)
    gated_rows = (
        alive_rows[:, None].astype(jnp.float32)
        * feat_query
        * (conv_wide + gain_rows[:, None] * widened)
    ).astype(jnp.bfloat16)
    return lax.all_to_all(gated_rows, "seq", split_axis=1, concat_axis=0, tiled=True)


def solution(mesh):
    in_specs = (
        P("tp", "seq"),
        P("tp", "seq"),
        P("tp", "seq"),
        P(None, "tp", None),
        P("tp", "seq"),
        P("tp"),
        P("tp"),
    )
    out_specs = P("tp", "seq")
    return jax.shard_map(shards, mesh=mesh, in_specs=in_specs, out_specs=out_specs, check_vma=False)
```

profile of v0, /device:TPU:24, one launch (start us, length us, event | category | flops | bytes accessed | tf_op | source)
XLA Modules:
  0.0 172.4 jit_solution(10389147794673392032)
XLA Ops:
  0.0 18.1 %all-to-all-start.2 = ((bf16[32,8,512]{2,1,0:T(8,128)(2,1)}), bf16[32,8,512]{2,1,0:T(8,128)(2,1)S(1)}, u32[]{:S(2)}, u32[]{:S(2)}) async-start(bf16[32,8,512]{2,1,0:T(8,128)(2,1)} %bitcast.127), calls=%async_computation.2 | async-start | bytes 524288 | tf_op jit(solution)/shard_map/all_to_all | solution.py:92
  21.5 18.4 %all-to-all-done.2 = bf16[32,8,512]{2,1,0:T(8,128)(2,1)S(1)} async-done(((bf16[32,8,512]{2,1,0:T(8,128)(2,1)}), bf16[32,8,512]{2,1,0:T(8,128)(2,1)S(1)}, u32[]{:S(2)}, u32[]{:S(2)}) %all-to-all-start.2) | async-done | bytes 262176 | tf_op jit(solution)/shard_map/all_to_all | solution.py:92
  40.0 4.8 %all-to-all-start.1 = ((bf16[32,8,512]{2,1,0:T(8,128)(2,1)}), bf16[32,8,512]{2,1,0:T(8,128)(2,1)S(1)}, u32[]{:S(2)}, u32[]{:S(2)}) async-start(bf16[32,8,512]{2,1,0:T(8,128)(2,1)} %bitcast.9), calls=%async_computation.1 | async-start | bytes 524288 | tf_op jit(solution)/shard_map/all_to_all | solution.py:91
  44.9 21.0 %all-to-all-done.1 = bf16[32,8,512]{2,1,0:T(8,128)(2,1)S(1)} async-done(((bf16[32,8,512]{2,1,0:T(8,128)(2,1)}), bf16[32,8,512]{2,1,0:T(8,128)(2,1)S(1)}, u32[]{:S(2)}, u32[]{:S(2)}) %all-to-all-start.1) | async-done | bytes 262176 | tf_op jit(solution)/shard_map/all_to_all | solution.py:91
  65.9 4.8 %all-to-all-start = ((bf16[32,8,512]{2,1,0:T(8,128)(2,1)}), bf16[32,8,512]{2,1,0:T(8,128)(2,1)S(1)}, u32[]{:S(2)}, u32[]{:S(2)}) async-start(bf16[32,8,512]{2,1,0:T(8,128)(2,1)} %bitcast.2), calls=%async_computation | async-start | bytes 524288 | tf_op jit(solution)/shard_map/all_to_all | solution.py:90
  71.5 0.9 fusion
  72.4 0.9 convolution_bitcast_fusion
  73.3 1.2 fusion.36
  74.6 2.2 %convolution_add_fusion.2 = f32[8,256,128]{2,1,0:T(8,128)} fusion(f32[8,256,128]{2,1,0:T(8,128)S(1)} %fusion.36, f32[8,256,128]{1,2,0:T(8,128)S(1)} %convolution_bitcast_fusion, f32[8,256,128]{1,2,0:T(8,128)S(1)} %fusion, f32[256,128]{0,1:T(8,128)S(1)} %copy.34, f32[256,128]{0,1:T(8,128)S(1)} %copy.32), kind=kOutput, calls=%fused_computation.9 | convolution fusion | flops 202604544 | bytes 4456448 | tf_op jit(solution)/shard_map/rka,aj->rkj/dot_general | solution.py:28
  76.8 14.8 %all-to-all-done = bf16[32,8,512]{2,1,0:T(8,128)(2,1)S(1)} async-done(((bf16[32,8,512]{2,1,0:T(8,128)(2,1)}), bf16[32,8,512]{2,1,0:T(8,128)(2,1)S(1)}, u32[]{:S(2)}, u32[]{:S(2)}) %all-to-all-start) | async-done | bytes 262176 | tf_op jit(solution)/shard_map/all_to_all | solution.py:90
  91.5 0.9 broadcast_in_dim.8
  92.4 4.9 %all-to-all-start.3 = ((f32[32,8,512]{2,1,0:T(8,128)}), f32[32,8,512]{2,1,0:T(8,128)S(1)}, u32[]{:S(2)}, u32[]{:S(2)}) async-start(f32[32,8,512]{2,1,0:T(8,128)} %broadcast_in_dim.8), calls=%async_computation.3 | async-start | bytes 1048576 | tf_op jit(solution)/shard_map/all_to_all | solution.py:88
  97.4 2.2 %fusion.37 = f32[8,256,128]{2,1,0:T(8,128)} fusion(f32[8,256,128]{1,2,0:T(8,128)S(1)} %convolution_bitcast_fusion, f32[8,256,128]{1,2,0:T(8,128)S(1)} %fusion, f32[256,128]{0,1:T(8,128)S(1)} %copy.34, f32[256,128]{0,1:T(8,128)S(1)} %copy.32), kind=kOutput, calls=%fused_computation.66 | convolution fusion | flops 202342400 | bytes 3407872 | tf_op jit(solution)/shard_map/rka,aj->rkj/dot_general | solution.py:28
  99.7 29.4 %all-to-all-done.3 = f32[32,8,512]{2,1,0:T(8,128)S(1)} async-done(((f32[32,8,512]{2,1,0:T(8,128)}), f32[32,8,512]{2,1,0:T(8,128)S(1)}, u32[]{:S(2)}, u32[]{:S(2)}) %all-to-all-start.3) | async-done | bytes 524320 | tf_op jit(solution)/shard_map/all_to_all | solution.py:88
  129.1 1.1 copy.37
  130.2 1.1 reshape.69
  131.3 1.0 fusion.49
  132.3 1.0 convolution_negate_fusion.1
  133.3 0.8 fusion.4
  134.2 0.8 fusion.8
  135.0 0.9 convolution_subtract_fusion.1
  136.0 0.9 convolution_add_fusion.1
  137.5 1.3 multiply_subtract_fusion
  138.9 0.8 fusion.73
  139.7 0.8 fusion.75
  140.6 0.9 convolution_add_fusion
  141.4 0.9 convolution_subtract_fusion
  142.3 1.3 fusion.13
  143.6 1.1 fusion.3
  145.1 0.7 copy-done.5
  146.3 25.4 %all_to_all.89 = bf16[8,32,512]{2,0,1:T(8,128)(2,1)S(1)} all-to-all(bf16[8,32,512]{2,0,1:T(8,128)(2,1)S(1)} %bitcast.124), channel_id=1, replica_groups=mesh['seq'=32,'tp'=16] {'seq'}, dimensions={1} | all-to-all | bytes 524288 | tf_op jit(solution)/shard_map/all_to_all | solution.py:112
  171.7 0.7 copy.68
  (44 shorter events, 5.8 us)
Async XLA Ops:
  0.0 18.1 %copy-start.8 = (f32[16,512]{1,0:T(8,128)S(1)}, f32[16,512]{1,0:T(8,128)}, u32[]{:S(2)}) copy-start(f32[16,512]{1,0:T(8,128)} %param.11) | copy-start | bytes 98308
  0.0 40.0 %all-to-all-start.2 = ((bf16[32,8,512]{2,1,0:T(8,128)(2,1)}), bf16[32,8,512]{2,1,0:T(8,128)(2,1)S(1)}, u32[]{:S(2)}, u32[]{:S(2)}) async-start(bf16[32,8,512]{2,1,0:T(8,128)(2,1)} %bitcast.127), calls=%async_computation.2 | async-start | bytes 524288 | tf_op jit(solution)/shard_map/all_to_all | solution.py:92
  18.7 0.7 copy-start
  19.4 2.1 %copy-start.9 = (f32[3,256,3]{1,2,0:T(4,128)S(1)}, f32[3,256,3]{1,2,0:T(4,128)}, u32[]{:S(2)}) copy-start(f32[3,256,3]{1,2,0:T(4,128)} %param.10) | copy-start | bytes 27652
  19.5 0.7 copy-start.12
  20.2 0.7 copy-start.13
  40.0 26.0 %all-to-all-start.1 = ((bf16[32,8,512]{2,1,0:T(8,128)(2,1)}), bf16[32,8,512]{2,1,0:T(8,128)(2,1)S(1)}, u32[]{:S(2)}, u32[]{:S(2)}) async-start(bf16[32,8,512]{2,1,0:T(8,128)(2,1)} %bitcast.9), calls=%async_computation.1 | async-start | bytes 524288 | tf_op jit(solution)/shard_map/all_to_all | solution.py:91
  65.9 25.6 %all-to-all-start = ((bf16[32,8,512]{2,1,0:T(8,128)(2,1)}), bf16[32,8,512]{2,1,0:T(8,128)(2,1)S(1)}, u32[]{:S(2)}, u32[]{:S(2)}) async-start(bf16[32,8,512]{2,1,0:T(8,128)(2,1)} %bitcast.2), calls=%async_computation | async-start | bytes 524288 | tf_op jit(solution)/shard_map/all_to_all | solution.py:90
  71.4 1.0 copy-start.4
  91.5 0.9 copy-start.6
  92.4 36.6 %all-to-all-start.3 = ((f32[32,8,512]{2,1,0:T(8,128)}), f32[32,8,512]{2,1,0:T(8,128)S(1)}, u32[]{:S(2)}, u32[]{:S(2)}) async-start(f32[32,8,512]{2,1,0:T(8,128)} %broadcast_in_dim.8), calls=%async_computation.3 | async-start | bytes 1048576 | tf_op jit(solution)/shard_map/all_to_all | solution.py:88
  97.4 2.2 %copy-start.7 = (bf16[32,8,512]{2,1,0:T(8,128)(2,1)S(1)}, bf16[32,8,512]{2,1,0:T(8,128)(2,1)}, u32[]{:S(2)}) copy-start(bf16[32,8,512]{2,1,0:T(8,128)(2,1)} %copy-done.6) | copy-start | bytes 786436
  132.3 1.0 copy-start.1
  136.0 1.2 copy-start.2
  136.0 1.5 copy-start.3
  144.9 1.0 copy-start.5
  145.1 0.8 copy-start.10
  145.1 0.8 copy-start.11
where the time goes:
time: 174 us; the launch traced here: 172 us
  waiting for transfers between devices  83.6 us (48%)
  starting transfers between devices  32.5 us (19%)
  blocking collectives  25.4 us (15%)
  matrix products  20.2 us (12%)
  local copies, waits for them, and re-layouts  7.77 us (4%)
  other arithmetic  2.53 us (1%)
    all_to_all x1, waiting for transfers between devices, shards(): lax.all_to_all(channel_rows, 'seq', split_axis=0, concat_axis=1, tiled=True)  29.4 us
    all_to_all x1, blocking collectives, shards(): lax.all_to_all(gated_rows, 'seq', split_axis=1, concat_axis=0, tiled=True)  25.4 us
    all_to_all x1, waiting for transfers between devices, shards(): lax.all_to_all(stream_k, 'seq', split_axis=0, concat_axis=1, tiled=True)  21 us
    dot_general x18, matrix products, contract(): return jnp.einsum(form, left, right, precision=precise)  20.2 us
    all_to_all x1, waiting for transfers between devices, shards(): lax.all_to_all(stream_v, 'seq', split_axis=0, concat_axis=1, tiled=True)  18.4 us
    all_to_all x1, starting transfers between devices, shards(): lax.all_to_all(stream_v, 'seq', split_axis=0, concat_axis=1, tiled=True)  18.1 us
    all_to_all x1, waiting for transfers between devices, shards(): lax.all_to_all(stream_q, 'seq', split_axis=0, concat_axis=1, tiled=True)  14.8 us
    all_to_all x1, starting transfers between devices, shards(): lax.all_to_all(channel_rows, 'seq', split_axis=0, concat_axis=1, tiled=True)  4.93 us
  transfers between devices with their start and end apart: 4, of which 4 were waited for; matrix products, arithmetic and copies ran while one was open for 6% of the time, Pallas kernels for 0%

commit v1 on v0

v1 whole, which is shorter than its diff:
```python
import jax
import jax.numpy as jnp
from jax import lax
from jax.experimental import pallas as pl
from jax.experimental.pallas import tpu as pltpu
from jax.sharding import PartitionSpec as P

f32, bf16 = jnp.float32, jnp.bfloat16
PEERS = 32
OWN = 8
BLOCK = 512
LANES = 128
TILES = BLOCK // LANES
VMEM = pl.BlockSpec(memory_space=pltpu.VMEM)


def lanes_of(shape):
    return lax.broadcasted_iota(jnp.int32, shape, 1)


def rows_of(shape):
    return lax.broadcasted_iota(jnp.int32, shape, 0)


def features(signal, taps):
    return (
        taps[:, 0:1] * signal
        + taps[:, 1:2] * pltpu.roll(signal, 1, 1)
        + taps[:, 2:3] * pltpu.roll(signal, 2, 1)
    )


def message_kernel(q_ref, k_ref, v_ref, taps_ref, filt_ref, out_ref):
    lane = lanes_of((16, LANES))
    small_row = rows_of((8, LANES))
    for chunk in range(PEERS // 2):
        rows = slice(16 * chunk, 16 * chunk + 16)
        key = k_ref[rows, :].astype(f32)
        value = v_ref[rows, :].astype(f32)
        feat_key = features(key, taps_ref[1, rows, :])
        feat_value = features(value, taps_ref[2, rows, :])
        product = (feat_key * feat_value).astype(bf16)
        q_first = q_ref[rows, 0:LANES].astype(f32)
        q_last = q_ref[rows, BLOCK - LANES:].astype(f32)

        def ends(first, last, place):
            return pltpu.roll(jnp.where(lane >= 64, last, first), place, 1)

        k_ends = ends(key[:, 0:LANES], key[:, BLOCK - LANES:], 2)
        v_ends = ends(value[:, 0:LANES], value[:, BLOCK - LANES:], 6)
        q_ends = ends(q_first, q_last, 10)
        wide = jnp.where(small_row < 2, filt_ref[chunk:chunk + 1, 0:LANES],
                         jnp.where(small_row < 4, filt_ref[chunk:chunk + 1, LANES:2 * LANES],
                                   jnp.where(small_row < 6, filt_ref[chunk:chunk + 1, 2 * LANES:3 * LANES],
                                             filt_ref[chunk:chunk + 1, 3 * LANES:4 * LANES])))
        lags = jnp.where(small_row % 2 == 1, wide, pltpu.roll(wide, 64, 1))
        lags = jnp.concatenate((lags, lags), axis=0)
        edge = jnp.where(lane < 4, k_ends, jnp.where(lane < 8, v_ends, jnp.where(lane < 12, q_ends, lags)))
        edge = edge.astype(bf16)
        for half in range(2):
            peer = 2 * chunk + half
            part = slice(8 * half, 8 * half + 8)
            for tile in range(TILES):
                out_ref[peer, tile] = product[part, LANES * tile:LANES * (tile + 1)]
            out_ref[peer, TILES] = edge[part]


def gate_kernel(q_ref, k_ref, v_ref, taps_ref, live_ref, gain_ref, query_ref, skip_ref):
    for chunk in range(PEERS // 2):
        rows = slice(16 * chunk, 16 * chunk + 16)
        feat_query = features(q_ref[rows, :].astype(f32), taps_ref[0, rows, :])
        feat_key = features(k_ref[rows, :].astype(f32), taps_ref[1, rows, :])
        feat_value = features(v_ref[rows, :].astype(f32), taps_ref[2, rows, :])
        product = (feat_key * feat_value).astype(bf16).astype(f32)
        query_ref[rows, :] = live_ref[rows, :] * feat_query
        skip_ref[rows, :] = gain_ref[rows, :] * product


DEPTH = 4
STEPS = 64 // DEPTH


def conv_kernel(msg_ref, aux_ref, out_ref, lag_ref, toep_ref, rows_ref, left_ref, sum_ref):
    lane = lanes_of((256, LANES))
    pad = 8 * (DEPTH - 1)
    edge = msg_ref[:, TILES].astype(f32).reshape(256, LANES)
    lag_ref[...] = jnp.where(lane < 64, pltpu.roll(edge, 64, 1), pltpu.roll(edge, 255, 0))

    earlier = jnp.concatenate((jnp.zeros((8, LANES), f32), edge[:-8]), axis=0)
    joined = jnp.where(lane % 4 < 2, earlier, edge)

    def spread(index):
        return jnp.concatenate([aux_ref[index]] * PEERS, axis=0)

    feat = (
        spread(0) * joined
        + spread(1) * pltpu.roll(joined, 1, 1)
        + spread(2) * pltpu.roll(joined, 2, 1)
    )
    first_product = pltpu.roll(feat * pltpu.roll(feat, LANES - 4, 1), LANES - 2, 1)
    first_product = first_product.astype(bf16).astype(f32)
    first_query = pltpu.roll(feat, LANES - 10, 1)

    rows_ref[0:pad, :] = jnp.zeros((pad, 256), f32)
    for peer in range(PEERS):
        for tile in range(TILES):
            part = msg_ref[peer, tile].astype(f32)
            if tile == 0:
                part = jnp.where(lane[:8] < 2, first_product[8 * peer:8 * peer + 8], part)
            start = pad + 16 * peer + 8 * (tile // 2)
            rows_ref[start:start + 8, LANES * (tile % 2):LANES * (tile % 2 + 1)] = part
    for back in range(DEPTH):
        left_ref[:, 256 * back:256 * (back + 1)] = rows_ref[pad - 8 * back:pad - 8 * back + 512, :].astype(bf16)

    lower = lanes_of((LANES, LANES)) >= rows_of((LANES, LANES))
    toep_ref[0] = jnp.zeros((LANES, LANES), bf16)
    turned = jnp.zeros((LANES, LANES), f32)
    for step in range(STEPS):
        for e in range(2 * DEPTH * step, 2 * DEPTH * (step + 1)):
            before = turned
            row = jnp.broadcast_to(lag_ref[2 * e:2 * e + 1, :], (LANES, LANES))
            turned = pltpu.roll(row, 0, 1, stride=1, stride_axis=0)
            toep_ref[e + 1] = jnp.where(lower, turned, before).astype(bf16)
        first = DEPTH * step
        parts = []
        for back in range(DEPTH):
            for half in range(2):
                at = 1 + 2 * (first + back) - half
                parts.append(jnp.concatenate((toep_ref[at], toep_ref[at + 1]), axis=1))
        right = jnp.concatenate(parts, axis=0)
        offset = 8 * first
        got = jnp.dot(left_ref[0:512 - offset, :], right, preferred_element_type=f32)
        if step == 0:
            sum_ref[...] = got
        else:
            sum_ref[offset:, :] += got

    for peer in range(PEERS):
        for half in range(2):
            start = 16 * peer + 8 * half
            result = sum_ref[start:start + 8, :].astype(bf16)
            if half == 0:
                group = slice(8 * peer, 8 * peer + 8)
                head = result[:, 0:LANES].astype(f32)
                done = aux_ref[3] * first_query[group] * (head + aux_ref[4] * first_product[group])
                head = jnp.where(lane[:8] < 2, done, head).astype(bf16)
                out_ref[peer, :, 0:LANES] = head
                out_ref[peer, :, LANES:256] = result[:, LANES:]
            else:
                out_ref[peer, :, 256:512] = result


def shards(stream_q, stream_k, stream_v, short_taps, filters, live_mask, skip_gain):
    message = pl.pallas_call(
        message_kernel,
        out_shape=jax.ShapeDtypeStruct((PEERS, TILES + 1, 8, LANES), bf16),
        in_specs=[VMEM] * 5,
        out_specs=VMEM,
        compiler_params=pltpu.CompilerParams(vmem_limit_bytes=16 << 20),
        name="message",
    )(stream_q, stream_k, stream_v, short_taps, filters)
    arrived = lax.all_to_all(message, "seq", split_axis=0, concat_axis=0, tiled=True)

    live = live_mask.astype(f32)
    query, skip = pl.pallas_call(
        gate_kernel,
        out_shape=[jax.ShapeDtypeStruct((256, BLOCK), f32)] * 2,
        in_specs=[VMEM] * 6,
        out_specs=[VMEM] * 2,
        compiler_params=pltpu.CompilerParams(vmem_limit_bytes=16 << 20),
        cost_estimate=pl.CostEstimate(flops=4000000, bytes_accessed=2 << 20, transcendentals=0),
        name="gate",
    )(stream_q, stream_k, stream_v, short_taps, live[:, None], skip_gain[:, None])

    offset = lax.axis_index("seq") * OWN
    own_taps = lax.dynamic_slice_in_dim(short_taps, offset, OWN, 1)
    own_live = lax.dynamic_slice_in_dim(live, offset, OWN, 0)
    own_gain = lax.dynamic_slice_in_dim(skip_gain, offset, OWN, 0)
    by_tap = jnp.transpose(own_taps, (2, 1, 0))
    kind = lax.broadcasted_iota(jnp.int32, (3, OWN, LANES), 2) // 4
    weights = jnp.where(kind == 0, by_tap[:, :, 1:2], jnp.where(kind == 1, by_tap[:, :, 2:3], by_tap[:, :, 0:1]))
    aux = jnp.concatenate(
        (
            weights,
            jnp.broadcast_to(own_live[None, :, None], (1, OWN, LANES)),
            jnp.broadcast_to(own_gain[None, :, None], (1, OWN, LANES)),
        ),
        axis=0,
    )

    convolved = pl.pallas_call(
        conv_kernel,
        out_shape=jax.ShapeDtypeStruct((PEERS, OWN, BLOCK), bf16),
        in_specs=[VMEM] * 2,
        out_specs=VMEM,
        scratch_shapes=[
            pltpu.VMEM((256, LANES), f32),
            pltpu.VMEM((129, LANES, LANES), bf16),
            pltpu.VMEM((512 + 8 * (DEPTH - 1), 256), f32),
            pltpu.VMEM((512, 256 * DEPTH), bf16),
            pltpu.VMEM((512, 256), f32),
        ],
        compiler_params=pltpu.CompilerParams(vmem_limit_bytes=32 << 20),
        cost_estimate=pl.CostEstimate(flops=2300000000, bytes_accessed=1 << 20, transcendentals=0),
        name="conv",
    )(arrived, aux)
    back = lax.all_to_all(convolved, "seq", split_axis=0, concat_axis=0, tiled=True)
    back = back.reshape(256, BLOCK).astype(f32)
    column = lax.broadcasted_iota(jnp.int32, (256, BLOCK), 1)
    return jnp.where(column < 2, back, query * (back + skip)).astype(bf16)


def solution(mesh):
    in_specs = (
        P("tp", "seq"),
        P("tp", "seq"),
        P("tp", "seq"),
        P(None, "tp", None),
        P("tp", "seq"),
        P("tp"),
        P("tp"),
    )
    return jax.shard_map(shards, mesh=mesh, in_specs=in_specs, out_specs=P("tp", "seq"), check_vma=False)
```

time: 174 us -> 78.5 us (0.45)
  waiting for transfers between devices: 83.6 us -> 42.5 us
  blocking collectives: 25.4 us -> 0 us
  matrix products: 20.2 us -> 0 us
  starting transfers between devices: 32.5 us -> 23 us
  Pallas kernels: 0 us -> 6.66 us
  local copies, waits for them, and re-layouts: 7.77 us -> 4.84 us
    all_to_all x4 -> x2, waiting for transfers between devices: 83.6 us -> 42.5 us  [the longest x1 23.5 us: shards(): lax.all_to_all(message, 'seq', split_axis=0, concat_axis=0, tiled=True)]
    all_to_all x1 -> x0, blocking collectives: 25.4 us -> none  [shards(): lax.all_to_all(gated_rows, 'seq', split_axis=1, concat_axis=0, tiled=True)]
    dot_general x18 -> x0, matrix products: 20.2 us -> none  [contract(): return jnp.einsum(form, left, right, precision=precise)]
    all_to_all x4 -> x2, starting transfers between devices: 32.5 us -> 23 us  [the longest x1 18.1 us: shards(): lax.all_to_all(message, 'seq', split_axis=0, concat_axis=0, tiled=True)]
    pallas_call x0 -> x3, Pallas kernels: none -> 6.66 us  [the longest x1 3.86 us: shards(): pl.pallas_call(conv_kernel, out_shape=jax.ShapeDtypeStruct((PEERS, OWN, B...]
    unnamed x30 -> x19, local copies, waits for them, and re-layouts: 3.52 us -> 4.19 us
  transfers between devices with their start and end apart: 4 -> 2, of which waited for: 4 -> 2; matrix products, arithmetic and copies ran while one was open for 6% -> 1% of each run, Pallas kernels for 0% -> 2%
where the time goes in v1:
time: 78.5 us; the launch traced here: 78 us
  waiting for transfers between devices  42.5 us (54%)
  starting transfers between devices  23 us (29%)
  Pallas kernels  6.66 us (8%)
  local copies, waits for them, and re-layouts  4.84 us (6%)
  other arithmetic  0.95 us (1%)
    all_to_all x1, waiting for transfers between devices, shards(): lax.all_to_all(message, 'seq', split_axis=0, concat_axis=0, tiled=True)  23.5 us
    all_to_all x1, waiting for transfers between devices, shards(): lax.all_to_all(convolved, 'seq', split_axis=0, concat_axis=0, tiled=True)  19 us
    all_to_all x1, starting transfers between devices, shards(): lax.all_to_all(message, 'seq', split_axis=0, concat_axis=0, tiled=True)  18.1 us
    all_to_all x1, starting transfers between devices, shards(): lax.all_to_all(convolved, 'seq', split_axis=0, concat_axis=0, tiled=True)  4.94 us
    unnamed x19, local copies, waits for them, and re-layouts  4.19 us
    pallas_call x1, Pallas kernels, shards(): pl.pallas_call(conv_kernel, out_shape=jax.ShapeDtypeStruct((PEERS, OWN, B...  3.86 us
    pallas_call x1, Pallas kernels, shards(): pl.pallas_call(message_kernel, out_shape=jax.ShapeDtypeStruct((PEERS, TIL...  1.58 us
  transfers between devices with their start and end apart: 2, of which 2 were waited for; matrix products, arithmetic and copies ran while one was open for 1% of the time, Pallas kernels for 2%

profile of v1, /device:TPU:24, one launch (start us, length us, event | category | flops | bytes accessed | tf_op | source)
XLA Modules:
  0.0 78.0 jit_solution(7226804888805216724)
XLA Ops:
  0.0 0.0 copy-start
  0.0 0.0 copy-start.5
  0.0 0.9 %copy.10.taps_ref = f32[3,256,3]{2,1,0:T(8,128)S(1)} copy(f32[3,256,3]{1,2,0:T(4,128)} %param.10) | data formatting | bytes 18432 | tf_op args[3]
  0.9 0.0 copy-done
  1.0 0.0 copy-done.5
  1.0 0.0 copy-start.1
  1.0 0.9 %copy-done.1 = bf16[256,512]{1,0:T(8,128)(2,1)S(1)} copy-done((bf16[256,512]{1,0:T(8,128)(2,1)S(1)}, bf16[256,512]{1,0:T(8,128)(2,1)}, u32[]{:S(2)}) %copy-start.1) | copy-done | bytes 262168
  1.9 0.9 %copy-done.3 = bf16[256,512]{1,0:T(8,128)(2,1)S(1)} copy-done((bf16[256,512]{1,0:T(8,128)(2,1)S(1)}, bf16[256,512]{1,0:T(8,128)(2,1)}, u32[]{:S(2)}) %copy-start.3) | copy-done | bytes 262168
  2.9 1.6 %message.1 = bf16[32,5,8,128]{3,2,1,0:T(8,128)(2,1)} custom-call(bf16[256,512]{1,0:T(8,128)(2,1)S(1)} %copy-done, bf16[256,512]{1,0:T(8,128)(2,1)S(1)} %copy-done.1, bf16[256,512]{1,0:T(8,128)(2,1)S(1)} %copy-done.3, f32[3,256,3]{2,1,0:T(8,128)S(1)} %copy.10.taps_ref, f32[16,512]{1,0:T(8,128)S(1)} %copy-done.5), custom_call_target="tpu_custom_call" | custom-call | tf_op jit(solution)/shard_map/message/pallas_call | solution.py:154
  4.5 18.1 %all-to-all-start = ((bf16[32,5,8,128]{3,2,1,0:T(8,128)(2,1)}), bf16[32,5,8,128]{3,2,1,0:T(8,128)(2,1)S(1)}, u32[]{:S(2)}, u32[]{:S(2)}) async-start(bf16[32,5,8,128]{3,2,1,0:T(8,128)(2,1)} %message.1), calls=%async_computation | async-start | bytes 655360 | tf_op jit(solution)/shard_map/all_to_all | solution.py:162
  22.5 0.0 copy-start.6
  22.6 0.0 copy-done.8
  22.6 0.0 copy-start.7
  22.6 0.7 copy-done.7
  23.3 0.1 dynamic_slice.11
  23.3 0.1 dynamic_slice.10
  23.4 0.0 copy-done.6
  23.4 0.1 dynamic-slice_bitcast_fusion
  23.5 0.1 select_select_fusion
  23.6 0.1 broadcast_in_dim.55
  23.7 0.1 broadcast_in_dim.54
  23.7 23.5 %all-to-all-done.msg_ref = bf16[32,5,8,128]{3,2,1,0:T(8,128)(2,1)S(1)} async-done(((bf16[32,5,8,128]{3,2,1,0:T(8,128)(2,1)}), bf16[32,5,8,128]{3,2,1,0:T(8,128)(2,1)S(1)}, u32[]{:S(2)}, u32[]{:S(2)}) %all-to-all-start) | async-done | bytes 327712 | tf_op jit(solution)/shard_map/all_to_all | solution.py:162
  47.2 3.9 %conv.1 = bf16[32,8,512]{2,1,0:T(8,128)(2,1)} custom-call(bf16[32,5,8,128]{3,2,1,0:T(8,128)(2,1)S(1)} %all-to-all-done.msg_ref, f32[5,8,128]{2,1,0:T(8,128)S(1)} %pad_maximum_fusion.aux_ref), custom_call_target="tpu_custom_call" | custom-call | flops 2300000000 | bytes 1048576 | tf_op jit(solution)/shard_map/conv/pallas_call | solution.py:191
  51.1 4.9 %all-to-all-start.1 = ((bf16[32,8,512]{2,1,0:T(8,128)(2,1)}), bf16[32,8,512]{2,1,0:T(8,128)(2,1)S(1)}, u32[]{:S(2)}, u32[]{:S(2)}) async-start(bf16[32,8,512]{2,1,0:T(8,128)(2,1)} %conv.1), calls=%async_computation.1 | async-start | bytes 524288 | tf_op jit(solution)/shard_map/all_to_all | solution.py:207
  56.0 0.0 copy-start.2
  56.0 0.1 copy.12.live_ref
  56.2 0.1 copy.13.gain_ref
  56.3 0.0 copy-done.4
  56.3 0.6 copy-done.2
  57.0 1.2 %gate.1 = (f32[256,512]{1,0:T(8,128)S(1)}, f32[256,512]{1,0:T(8,128)S(1)}) custom-call(bf16[256,512]{1,0:T(8,128)(2,1)S(1)} %copy-done, bf16[256,512]{1,0:T(8,128)(2,1)S(1)} %copy-done.2, bf16[256,512]{1,0:T(8,128)(2,1)S(1)} %copy-done.4, f32[3,256,3]{2,1,0:T(8,128)S(1)} %copy.10.taps_ref, f32[256,1]{1,0:T(8,128)S(1)} %copy.12.live_ref, ...), custom_call_target="tpu_custom_call" | custom-call | flops 4000000 | bytes 2097152 | tf_op jit(solution)/shard_map/gate/pallas_call | solution.py:165
  58.2 19.0 %all-to-all-done.1 = bf16[32,8,512]{2,1,0:T(8,128)(2,1)S(1)} async-done(((bf16[32,8,512]{2,1,0:T(8,128)(2,1)}), bf16[32,8,512]{2,1,0:T(8,128)(2,1)S(1)}, u32[]{:S(2)}, u32[]{:S(2)}) %all-to-all-start.1) | async-done | bytes 262176 | tf_op jit(solution)/shard_map/all_to_all | solution.py:207
  77.2 0.8 %fusion.1 = bf16[256,512]{1,0:T(8,128)(2,1)} fusion(f32[256,512]{1,0:T(8,128)S(1)} %get-tuple-element.7, f32[256,512]{1,0:T(8,128)S(1)} %get-tuple-element.8, bf16[32,8,512]{2,1,0:T(8,128)(2,1)S(1)} %all-to-all-done.1, pred[512]{0:T(512)(128)(4,1)S(1)} %iota_compare_fusion), kind=kLoop, calls=%fused_computation.3 | loop fusion | flops 655360 | bytes 1573376 | tf_op jit(solution)/shard_map/convert_element_type | solution.py:210
  (9 shorter events, 0.0 us)
Async XLA Ops:
  0.0 1.0 %copy-start = (bf16[256,512]{1,0:T(8,128)(2,1)S(1)}, bf16[256,512]{1,0:T(8,128)(2,1)}, u32[]{:S(2)}) copy-start(bf16[256,512]{1,0:T(8,128)(2,1)} %q_ref.3) | copy-start | bytes 786436
  0.0 1.0 %copy-start.5 = (f32[16,512]{1,0:T(8,128)S(1)}, f32[16,512]{1,0:T(8,128)}, u32[]{:S(2)}) copy-start(f32[16,512]{1,0:T(8,128)} %filt_ref.1) | copy-start | bytes 98308
  1.0 1.0 %copy-start.1 = (bf16[256,512]{1,0:T(8,128)(2,1)S(1)}, bf16[256,512]{1,0:T(8,128)(2,1)}, u32[]{:S(2)}) copy-start(bf16[256,512]{1,0:T(8,128)(2,1)} %k_ref.3) | copy-start | bytes 786436
  1.9 0.9 %copy-start.3 = (bf16[256,512]{1,0:T(8,128)(2,1)S(1)}, bf16[256,512]{1,0:T(8,128)(2,1)}, u32[]{:S(2)}) copy-start(bf16[256,512]{1,0:T(8,128)(2,1)} %v_ref.3) | copy-start | bytes 786436
  4.5 18.1 %copy-start.8 = (s32[256]{0:T(256)S(1)}, s32[256]{0:T(256)}, u32[]{:S(2)}) copy-start(s32[256]{0:T(256)} %param.12) | copy-start | bytes 3076
  4.5 42.7 %all-to-all-start = ((bf16[32,5,8,128]{3,2,1,0:T(8,128)(2,1)}), bf16[32,5,8,128]{3,2,1,0:T(8,128)(2,1)S(1)}, u32[]{:S(2)}, u32[]{:S(2)}) async-start(bf16[32,5,8,128]{3,2,1,0:T(8,128)(2,1)} %message.1), calls=%async_computation | async-start | bytes 655360 | tf_op jit(solution)/shard_map/all_to_all | solution.py:162
  22.5 0.9 %copy-start.6 = (f32[3,256,3]{1,2,0:T(4,128)S(1)}, f32[3,256,3]{1,2,0:T(4,128)}, u32[]{:S(2)}) copy-start(f32[3,256,3]{1,2,0:T(4,128)} %param.10) | copy-start | bytes 27652
  22.6 0.7 copy-start.7
  51.1 5.3 %copy-start.4 = (bf16[256,512]{1,0:T(8,128)(2,1)S(1)}, bf16[256,512]{1,0:T(8,128)(2,1)}, u32[]{:S(2)}) copy-start(bf16[256,512]{1,0:T(8,128)(2,1)} %v_ref.3) | copy-start | bytes 786436
  51.1 26.1 %all-to-all-start.1 = ((bf16[32,8,512]{2,1,0:T(8,128)(2,1)}), bf16[32,8,512]{2,1,0:T(8,128)(2,1)S(1)}, u32[]{:S(2)}, u32[]{:S(2)}) async-start(bf16[32,8,512]{2,1,0:T(8,128)(2,1)} %conv.1), calls=%async_computation.1 | async-start | bytes 524288 | tf_op jit(solution)/shard_map/all_to_all | solution.py:207
  56.0 1.0 %copy-start.2 = (bf16[256,512]{1,0:T(8,128)(2,1)S(1)}, bf16[256,512]{1,0:T(8,128)(2,1)}, u32[]{:S(2)}) copy-start(bf16[256,512]{1,0:T(8,128)(2,1)} %k_ref.3) | copy-start | bytes 786436

commit v2 on v1

v2 whole, which is shorter than its diff:
```python
import jax
import jax.numpy as jnp
from jax import lax
from jax.experimental import pallas as pl
from jax.experimental.pallas import tpu as pltpu
from jax.sharding import PartitionSpec as P

f32, bf16 = jnp.float32, jnp.bfloat16
PEERS = 32
OWN = 8
BLOCK = 512
LANES = 128
TILES = BLOCK // LANES
FIRST_OUT, FIRST_BACK = 22, 16
ORDER_OUT = [(place + FIRST_OUT) % PEERS for place in range(PEERS)]
ORDER_BACK = [(place + FIRST_BACK) % PEERS for place in range(PEERS)]


def place_there(group):
    return (group + FIRST_BACK - FIRST_OUT) % PEERS


def place_from(block):
    return (block - FIRST_OUT) % PEERS


def place_back(block):
    return (block - FIRST_BACK) % PEERS


def runs(places):
    found = []
    for place in sorted(places):
        if found and found[-1].stop == place:
            found[-1] = slice(found[-1].start, place + 1)
        else:
            found.append(slice(place, place + 1))
    return found


VMEM = pl.BlockSpec(memory_space=pltpu.VMEM)
HBM = pl.BlockSpec(memory_space=pltpu.HBM)


def lanes_of(shape):
    return lax.broadcasted_iota(jnp.int32, shape, 1)


def rows_of(shape):
    return lax.broadcasted_iota(jnp.int32, shape, 0)


def features(signal, taps):
    return (
        taps[:, 0:1] * signal
        + taps[:, 1:2] * pltpu.roll(signal, 1, 1)
        + taps[:, 2:3] * pltpu.roll(signal, 2, 1)
    )


def columns_of(rows):
    spare = 16 - sum(row.shape[0] for row in rows)
    return jnp.transpose(jnp.concatenate(list(rows) + [jnp.zeros((spare, 256), f32)], axis=0))


PARTS = 4
ROWS = 256 // PARTS


def message_kernel(q_hbm, k_hbm, v_hbm, taps_hbm, filt_hbm, out_hbm, qf, ql, kk, vv, taps_ref, filt_ref, out_ref, sems, out_sems):
    small = [
        pltpu.make_async_copy(taps_hbm, taps_ref, sems.at[0]),
        pltpu.make_async_copy(filt_hbm, filt_ref, sems.at[1]),
        pltpu.make_async_copy(q_hbm.at[:, 0:LANES], qf, sems.at[2]),
        pltpu.make_async_copy(q_hbm.at[:, BLOCK - LANES:], ql, sems.at[3]),
    ]
    small[0].start()
    loads = []
    for part in range(PARTS):
        span = slice(ROWS * part, ROWS * (part + 1))
        loads.append(
            (
                pltpu.make_async_copy(k_hbm.at[span], kk.at[span], sems.at[4 + 2 * part]),
                pltpu.make_async_copy(v_hbm.at[span], vv.at[span], sems.at[5 + 2 * part]),
            )
        )
        for copy in loads[-1]:
            copy.start()
        if part == 0:
            for copy in small[1:]:
                copy.start()
    small[0].wait()
    taps = columns_of((taps_ref[1], taps_ref[2]))
    lane = lanes_of((16, LANES))
    small_row = rows_of((8, LANES))
    stores = []
    for part in range(PARTS):
        for copy in loads[part]:
            copy.wait()
        if part == 0:
            for copy in small[1:]:
                copy.wait()
        for chunk in range(part * ROWS // 16, (part + 1) * ROWS // 16):
            rows = slice(16 * chunk, 16 * chunk + 16)
            key = kk[rows, :].astype(f32)
            value = vv[rows, :].astype(f32)
            feat_key = features(key, taps[rows, 0:3])
            feat_value = features(value, taps[rows, 3:6])
            product = (feat_key * feat_value).astype(bf16)

            def ends(first, last, place):
                return pltpu.roll(jnp.where(lane >= 64, last, first), place, 1)

            k_ends = ends(key[:, 0:LANES], key[:, BLOCK - LANES:], 2)
            v_ends = ends(value[:, 0:LANES], value[:, BLOCK - LANES:], 6)
            q_ends = ends(qf[rows, :].astype(f32), ql[rows, :].astype(f32), 10)
            wide = jnp.where(small_row < 2, filt_ref[chunk:chunk + 1, 0:LANES],
                             jnp.where(small_row < 4, filt_ref[chunk:chunk + 1, LANES:2 * LANES],
                                       jnp.where(small_row < 6, filt_ref[chunk:chunk + 1, 2 * LANES:3 * LANES],
                                                 filt_ref[chunk:chunk + 1, 3 * LANES:4 * LANES])))
            lags = jnp.where(small_row % 2 == 1, wide, pltpu.roll(wide, 64, 1))
            lags = jnp.concatenate((lags, lags), axis=0)
            edge = jnp.where(lane < 4, k_ends, jnp.where(lane < 8, v_ends, jnp.where(lane < 12, q_ends, lags)))
            edge = edge.astype(bf16)
            for half in range(2):
                peer = 2 * chunk + half
                piece = slice(8 * half, 8 * half + 8)
                for tile in range(TILES):
                    out_ref[place_there(peer), tile] = product[piece, LANES * tile:LANES * (tile + 1)]
                out_ref[place_there(peer), TILES] = edge[piece]
        for span in runs([place_there(part * PEERS // PARTS + peer) for peer in range(PEERS // PARTS)]):
            stores.append(pltpu.make_async_copy(out_ref.at[span], out_hbm.at[span], out_sems.at[len(stores)]))
            stores[-1].start()
    for copy in stores:
        copy.wait()


def gate_kernel(q_ref, k_ref, v_ref, taps_ref, live_ref, gain_ref, query_ref, skip_ref, aux_ref, table_ref):
    table_ref[...] = columns_of(
        (taps_ref[0], taps_ref[1], taps_ref[2], live_ref[...].astype(f32), gain_ref[...])
    )
    place = lax.rem(lax.axis_index("seq") + PEERS - FIRST_BACK, PEERS)
    own = table_ref[pl.ds(pl.multiple_of(place * OWN, OWN), OWN), :]
    kind = lanes_of((OWN, LANES)) // 4
    for tap in range(3):
        aux_ref[tap] = jnp.where(
            kind == 0, own[:, 3 + tap:4 + tap], jnp.where(kind == 1, own[:, 6 + tap:7 + tap], own[:, tap:tap + 1])
        )
    for place in range(2):
        aux_ref[3 + place] = jnp.broadcast_to(own[:, 9 + place:10 + place], (OWN, LANES))
    for chunk in range(PEERS // 2):
        rows = slice(16 * chunk, 16 * chunk + 16)
        taps = table_ref[rows, :]
        feat_query = features(q_ref[rows, :].astype(f32), taps[:, 0:3])
        feat_key = features(k_ref[rows, :].astype(f32), taps[:, 3:6])
        feat_value = features(v_ref[rows, :].astype(f32), taps[:, 6:9])
        product = (feat_key * feat_value).astype(bf16).astype(f32)
        query_ref[rows, :] = taps[:, 9:10] * feat_query
        skip_ref[rows, :] = taps[:, 10:11] * product


DEPTH = 4
STEPS = 64 // DEPTH


def conv_kernel(msg_ref, aux_ref, out_hbm, lag_ref, toep_ref, rows_ref, left_ref, sum_ref, out_ref, sems):
    lane = lanes_of((256, LANES))
    pad = 8 * (DEPTH - 1)
    edge = jnp.concatenate([msg_ref[place_from(block), TILES].astype(f32) for block in range(PEERS)], axis=0)
    lag_ref[...] = jnp.where(lane < 64, pltpu.roll(edge, 64, 1), pltpu.roll(edge, 255, 0))

    earlier = jnp.concatenate((jnp.zeros((8, LANES), f32), edge[:-8]), axis=0)
    joined = jnp.where(lane % 4 < 2, earlier, edge)

    def spread(index):
        return jnp.concatenate([aux_ref[index]] * PEERS, axis=0)

    feat = (
        spread(0) * joined
        + spread(1) * pltpu.roll(joined, 1, 1)
        + spread(2) * pltpu.roll(joined, 2, 1)
    )
    first_product = pltpu.roll(feat * pltpu.roll(feat, LANES - 4, 1), LANES - 2, 1)
    first_product = first_product.astype(bf16).astype(f32)
    first_query = pltpu.roll(feat, LANES - 10, 1)

    rows_ref[0:pad, :] = jnp.zeros((pad, 256), f32)
    for peer in range(PEERS):
        for tile in range(TILES):
            part = msg_ref[place_from(peer), tile].astype(f32)
            if tile == 0:
                part = jnp.where(lane[:8] < 2, first_product[8 * peer:8 * peer + 8], part)
            start = pad + 16 * peer + 8 * (tile // 2)
            rows_ref[start:start + 8, LANES * (tile % 2):LANES * (tile % 2 + 1)] = part
    for back in range(DEPTH):
        left_ref[:, 256 * back:256 * (back + 1)] = rows_ref[pad - 8 * back:pad - 8 * back + 512, :].astype(bf16)

    lower = lanes_of((LANES, LANES)) >= rows_of((LANES, LANES))
    toep_ref[0] = jnp.zeros((LANES, LANES), bf16)
    turned = jnp.zeros((LANES, LANES), f32)
    stores = []
    for step in range(STEPS):
        for e in range(2 * DEPTH * step, 2 * DEPTH * (step + 1)):
            before = turned
            row = jnp.broadcast_to(lag_ref[2 * e:2 * e + 1, :], (LANES, LANES))
            turned = pltpu.roll(row, 0, 1, stride=1, stride_axis=0)
            toep_ref[e + 1] = jnp.where(lower, turned, before).astype(bf16)
        first = DEPTH * step
        parts = []
        for back in range(DEPTH):
            for half in range(2):
                at = 1 + 2 * (first + back) - half
                parts.append(jnp.concatenate((toep_ref[at], toep_ref[at + 1]), axis=1))
        right = jnp.concatenate(parts, axis=0)
        offset = 8 * first
        got = jnp.dot(left_ref[0:512 - offset, :], right, preferred_element_type=f32)
        if step == 0:
            sum_ref[...] = got
        else:
            sum_ref[offset:, :] += got

        for peer in range(DEPTH // 2 * step, DEPTH // 2 * (step + 1)):
            group = slice(8 * peer, 8 * peer + 8)
            result = sum_ref[16 * peer:16 * peer + 16, :].astype(bf16)
            head = result[0:8, 0:LANES].astype(f32)
            done = aux_ref[3] * first_query[group] * (head + aux_ref[4] * first_product[group])
            out_ref[place_back(peer), :, 0:LANES] = jnp.where(lane[:8] < 2, done, head).astype(bf16)
            out_ref[place_back(peer), :, LANES:256] = result[0:8, LANES:]
            out_ref[place_back(peer), :, 256:512] = result[8:16]
        if step % 2:
            for span in runs([place_back(DEPTH // 2 * (step - 1) + peer) for peer in range(DEPTH)]):
                stores.append(pltpu.make_async_copy(out_ref.at[span], out_hbm.at[span], sems.at[len(stores)]))
                stores[-1].start()
    for copy in stores:
        copy.wait()


def shards(stream_q, stream_k, stream_v, short_taps, filters, live_mask, skip_gain):
    taps_wide = jnp.transpose(short_taps, (0, 2, 1))
    message = pl.pallas_call(
        message_kernel,
        out_shape=jax.ShapeDtypeStruct((PEERS, TILES + 1, 8, LANES), bf16),
        in_specs=[HBM] * 5,
        out_specs=HBM,
        scratch_shapes=[
            pltpu.VMEM((256, LANES), bf16),
            pltpu.VMEM((256, LANES), bf16),
            pltpu.VMEM((256, BLOCK), bf16),
            pltpu.VMEM((256, BLOCK), bf16),
            pltpu.VMEM((3, 3, 256), f32),
            pltpu.VMEM((16, BLOCK), f32),
            pltpu.VMEM((PEERS, TILES + 1, 8, LANES), bf16),
            pltpu.SemaphoreType.DMA((4 + 2 * PARTS,)),
            pltpu.SemaphoreType.DMA((2 * PARTS,)),
        ],
        name="message",
    )(stream_q, stream_k, stream_v, taps_wide, filters)
    arrived = lax.all_to_all(message, "seq", split_axis=0, concat_axis=0, tiled=True, axis_index_groups=[ORDER_OUT])

    query, skip, aux = pl.pallas_call(
        gate_kernel,
        out_shape=[jax.ShapeDtypeStruct((256, BLOCK), f32)] * 2 + [jax.ShapeDtypeStruct((5, OWN, LANES), f32)],
        in_specs=[VMEM] * 6,
        out_specs=[VMEM] * 3,
        scratch_shapes=[pltpu.VMEM((256, 16), f32)],
        compiler_params=pltpu.CompilerParams(vmem_limit_bytes=16 << 20),
        cost_estimate=pl.CostEstimate(flops=4000000, bytes_accessed=2 << 20, transcendentals=0),
        name="gate",
    )(stream_q, stream_k, stream_v, taps_wide, live_mask[None, :], skip_gain[None, :])

    convolved = pl.pallas_call(
        conv_kernel,
        out_shape=jax.ShapeDtypeStruct((PEERS, OWN, BLOCK), bf16),
        in_specs=[VMEM] * 2,
        out_specs=HBM,
        scratch_shapes=[
            pltpu.VMEM((256, LANES), f32),
            pltpu.VMEM((129, LANES, LANES), bf16),
            pltpu.VMEM((512 + 8 * (DEPTH - 1), 256), f32),
            pltpu.VMEM((512, 256 * DEPTH), bf16),
            pltpu.VMEM((512, 256), f32),
            pltpu.VMEM((PEERS, OWN, BLOCK), bf16),
            pltpu.SemaphoreType.DMA((STEPS,)),
        ],
        compiler_params=pltpu.CompilerParams(vmem_limit_bytes=32 << 20),
        cost_estimate=pl.CostEstimate(flops=2300000000, bytes_accessed=1 << 20, transcendentals=0),
        name="conv",
    )(arrived, aux)
    back = lax.all_to_all(convolved, "seq", split_axis=0, concat_axis=0, tiled=True, axis_index_groups=[ORDER_BACK])
    back = back.reshape(256, BLOCK).astype(f32)
    column = lax.broadcasted_iota(jnp.int32, (256, BLOCK), 1)
    return jnp.where(column < 2, back, query * (back + skip)).astype(bf16)


def solution(mesh):
    in_specs = (
        P("tp", "seq"),
        P("tp", "seq"),
        P("tp", "seq"),
        P(None, "tp", None),
        P("tp", "seq"),
        P("tp"),
        P("tp"),
    )
    return jax.shard_map(shards, mesh=mesh, in_specs=in_specs, out_specs=P("tp", "seq"), check_vma=False)
```

time: 78.5 us -> 71.6 us (0.912)
  waiting for transfers between devices: 42.5 us -> 30.2 us
  starting transfers between devices: 23 us -> 31.4 us
  local copies, waits for them, and re-layouts: 4.84 us -> 0.65 us
  Pallas kernels: 6.66 us -> 8.14 us
    all_to_all x2, waiting for transfers between devices: 42.5 us -> 30.2 us  [the longest x1 17.6 us: shards(): lax.all_to_all(message, 'seq', split_axis=0, concat_axis=0, tiled=True, a...]
    all_to_all x2, starting transfers between devices: 23 us -> 31.4 us  [the longest x1 18.9 us: shards(): lax.all_to_all(message, 'seq', split_axis=0, concat_axis=0, tiled=True, a...]
    unnamed x19 -> x12, local copies, waits for them, and re-layouts: 4.19 us -> 0.65 us
    pallas_call x1, Pallas kernels: 1.58 us -> 2.86 us  [shards(): pl.pallas_call(message_kernel, out_shape=jax.ShapeDtypeStruct((PEERS, TIL...]
  transfers between devices with their start and end apart: 2 -> 2, of which waited for: 2 -> 2; matrix products, arithmetic and copies ran while one was open for 1% -> 0% of each run, Pallas kernels for 2% -> 2%
where the time goes in v2:
time: 71.6 us; the launch traced here: 71.3 us
  starting transfers between devices  31.4 us (44%)
  waiting for transfers between devices  30.2 us (42%)
  Pallas kernels  8.14 us (11%)
  other arithmetic  0.85 us (1%)
    all_to_all x1, starting transfers between devices, shards(): lax.all_to_all(message, 'seq', split_axis=0, concat_axis=0, tiled=True, a...  18.9 us
    all_to_all x1, waiting for transfers between devices, shards(): lax.all_to_all(message, 'seq', split_axis=0, concat_axis=0, tiled=True, a...  17.6 us
    all_to_all x1, waiting for transfers between devices, shards(): lax.all_to_all(convolved, 'seq', split_axis=0, concat_axis=0, tiled=True,...  12.6 us
    all_to_all x1, starting transfers between devices, shards(): lax.all_to_all(convolved, 'seq', split_axis=0, concat_axis=0, tiled=True,...  12.5 us
    pallas_call x1, Pallas kernels, shards(): pl.pallas_call(conv_kernel, out_shape=jax.ShapeDtypeStruct((PEERS, OWN, B...  3.89 us
    pallas_call x1, Pallas kernels, shards(): pl.pallas_call(message_kernel, out_shape=jax.ShapeDtypeStruct((PEERS, TIL...  2.86 us
  transfers between devices with their start and end apart: 2, of which 2 were waited for; matrix products, arithmetic and copies ran while one was open for 0% of the time, Pallas kernels for 2%

profile of v2, /device:TPU:24, one launch (start us, length us, event | category | flops | bytes accessed | tf_op | source)
XLA Modules:
  0.0 71.3 jit_solution(13876638790909543721)
XLA Ops:
  0.0 0.0 copy-start.2
  0.0 2.9 %message.1 = bf16[32,5,8,128]{3,2,1,0:T(8,128)(2,1)} custom-call(bf16[256,512]{1,0:T(8,128)(2,1)} %q_ref.1, bf16[256,512]{1,0:T(8,128)(2,1)} %k_ref.1, bf16[256,512]{1,0:T(8,128)(2,1)} %v_ref.1, f32[3,3,256]{2,1,0:T(4,128)} %bitcast.6, f32[16,512]{1,0:T(8,128)} %filt_hbm.1), custom_call_target="tpu_custom_call" | custom-call | tf_op jit(solution)/shard_map/message/pallas_call | solution.py:240
  2.9 0.0 copy-start
  2.9 0.0 copy-start.1
  2.9 0.0 copy-start.3
  2.9 0.0 copy-start.5
  2.9 18.9 %all-to-all-start = ((bf16[32,5,8,128]{3,2,1,0:T(8,128)(2,1)}), bf16[32,5,8,128]{3,2,1,0:T(8,128)(2,1)S(1)}, u32[]{:S(2)}, u32[]{:S(2)}) async-start(bf16[32,5,8,128]{3,2,1,0:T(8,128)(2,1)} %message.1), calls=%async_computation | async-start | bytes 655360 | tf_op jit(solution)/shard_map/all_to_all | solution.py:258
  21.8 0.0 copy-start.4
  21.8 0.0 copy-done.2
  21.9 0.0 copy-done
  21.9 0.0 copy-done.1
  21.9 0.0 copy-done.3
  21.9 0.0 copy-done.5
  21.9 0.6 copy-done.4
  22.5 1.4 %gate.1 = (f32[256,512]{1,0:T(8,128)S(1)}, f32[256,512]{1,0:T(8,128)S(1)}, f32[5,8,128]{2,1,0:T(8,128)S(1)}) custom-call(bf16[256,512]{1,0:T(8,128)(2,1)S(1)} %copy-done, bf16[256,512]{1,0:T(8,128)(2,1)S(1)} %copy-done.1, bf16[256,512]{1,0:T(8,128)(2,1)S(1)} %copy-done.2, f32[3,3,256]{2,1,0:T(4,128)S(1)} %bitcast.7, s32[1,256]{1,0:T(1,128)S(1)} %bitcast.8, ...), custom_call_target="tpu_custom_call" | custom-call | flops 4000000 | bytes 2097152 | tf_op jit(solution)/shard_map/gate/pallas_call | solution.py:260
  23.9 17.6 %all-to-all-done.msg_ref = bf16[32,5,8,128]{3,2,1,0:T(8,128)(2,1)S(1)} async-done(((bf16[32,5,8,128]{3,2,1,0:T(8,128)(2,1)}), bf16[32,5,8,128]{3,2,1,0:T(8,128)(2,1)S(1)}, u32[]{:S(2)}, u32[]{:S(2)}) %all-to-all-start) | async-done | bytes 327712 | tf_op jit(solution)/shard_map/all_to_all | solution.py:258
  41.5 3.9 %conv.1 = bf16[32,8,512]{2,1,0:T(8,128)(2,1)} custom-call(bf16[32,5,8,128]{3,2,1,0:T(8,128)(2,1)S(1)} %all-to-all-done.msg_ref, f32[5,8,128]{2,1,0:T(8,128)S(1)} %get-tuple-element.8.aux_ref), custom_call_target="tpu_custom_call" | custom-call | flops 2300000000 | bytes 1048576 | tf_op jit(solution)/shard_map/conv/pallas_call | solution.py:271
  45.4 12.5 %all-to-all-start.1 = ((bf16[32,8,512]{2,1,0:T(8,128)(2,1)}), bf16[32,8,512]{2,1,0:T(8,128)(2,1)S(1)}, u32[]{:S(2)}, u32[]{:S(2)}) async-start(bf16[32,8,512]{2,1,0:T(8,128)(2,1)} %conv.1), calls=%async_computation.1 | async-start | bytes 524288 | tf_op jit(solution)/shard_map/all_to_all | solution.py:289
  57.9 12.6 %all-to-all-done.1 = bf16[32,8,512]{2,1,0:T(8,128)(2,1)S(1)} async-done(((bf16[32,8,512]{2,1,0:T(8,128)(2,1)}), bf16[32,8,512]{2,1,0:T(8,128)(2,1)S(1)}, u32[]{:S(2)}, u32[]{:S(2)}) %all-to-all-start.1) | async-done | bytes 262176 | tf_op jit(solution)/shard_map/all_to_all | solution.py:289
  70.5 0.8 %fusion.1 = bf16[256,512]{1,0:T(8,128)(2,1)} fusion(f32[256,512]{1,0:T(8,128)S(1)} %get-tuple-element.9, f32[256,512]{1,0:T(8,128)S(1)} %get-tuple-element.10, bf16[32,8,512]{2,1,0:T(8,128)(2,1)S(1)} %all-to-all-done.1, pred[512]{0:T(512)(128)(4,1)S(1)} %iota_compare_fusion), kind=kLoop, calls=%fused_computation.3 | loop fusion | flops 655360 | bytes 1573376 | tf_op jit(solution)/shard_map/convert_element_type | solution.py:292
  (1 shorter events, 0.0 us)
Async XLA Ops:
  0.0 21.8 %copy-start.2 = (bf16[256,512]{1,0:T(8,128)(2,1)S(1)}, bf16[256,512]{1,0:T(8,128)(2,1)}, u32[]{:S(2)}) copy-start(bf16[256,512]{1,0:T(8,128)(2,1)} %v_ref.1) | copy-start | bytes 786436
  2.9 19.0 %copy-start = (bf16[256,512]{1,0:T(8,128)(2,1)S(1)}, bf16[256,512]{1,0:T(8,128)(2,1)}, u32[]{:S(2)}) copy-start(bf16[256,512]{1,0:T(8,128)(2,1)} %q_ref.1) | copy-start | bytes 786436
  2.9 19.0 %copy-start.1 = (bf16[256,512]{1,0:T(8,128)(2,1)S(1)}, bf16[256,512]{1,0:T(8,128)(2,1)}, u32[]{:S(2)}) copy-start(bf16[256,512]{1,0:T(8,128)(2,1)} %k_ref.1) | copy-start | bytes 786436
  2.9 19.0 %copy-start.3 = (f32[3,256,3]{1,2,0:T(4,128)S(1)}, f32[3,256,3]{1,2,0:T(4,128)}, u32[]{:S(2)}) copy-start(f32[3,256,3]{1,2,0:T(4,128)} %param.10) | copy-start | bytes 27652
  2.9 19.0 %copy-start.5 = (f32[256]{0:T(256)S(1)}, f32[256]{0:T(256)}, u32[]{:S(2)}) copy-start(f32[256]{0:T(256)} %param.13) | copy-start | bytes 3076
  2.9 38.6 %all-to-all-start = ((bf16[32,5,8,128]{3,2,1,0:T(8,128)(2,1)}), bf16[32,5,8,128]{3,2,1,0:T(8,128)(2,1)S(1)}, u32[]{:S(2)}, u32[]{:S(2)}) async-start(bf16[32,5,8,128]{3,2,1,0:T(8,128)(2,1)} %message.1), calls=%async_computation | async-start | bytes 655360 | tf_op jit(solution)/shard_map/all_to_all | solution.py:258
  21.8 0.7 copy-start.4
  45.4 25.1 %all-to-all-start.1 = ((bf16[32,8,512]{2,1,0:T(8,128)(2,1)}), bf16[32,8,512]{2,1,0:T(8,128)(2,1)S(1)}, u32[]{:S(2)}, u32[]{:S(2)}) async-start(bf16[32,8,512]{2,1,0:T(8,128)(2,1)} %conv.1), calls=%async_computation.1 | async-start | bytes 524288 | tf_op jit(solution)/shard_map/all_to_all | solution.py:289

commit v3 on v2

v3 whole, which is shorter than its diff:
```python
import jax
import jax.numpy as jnp
from jax import lax
from jax.experimental import pallas as pl
from jax.experimental.pallas import tpu as pltpu
from jax.sharding import PartitionSpec as P

f32, bf16 = jnp.float32, jnp.bfloat16
PEERS = 32
OWN = 8
BLOCK = 512
LANES = 128
TILES = BLOCK // LANES
FIRST_OUT, FIRST_BACK = 22, 16
ORDER_OUT = [(FIRST_OUT + place) % PEERS for place in range(PEERS)]
ORDER_BACK = [(FIRST_BACK + place) % PEERS for place in range(PEERS)]


def own_group(index):
    return lax.rem(index + PEERS - FIRST_BACK, PEERS)


def place_there(group):
    return ORDER_OUT.index(ORDER_BACK[group])


def place_from(block):
    return ORDER_OUT.index(block)


def place_back(block):
    return ORDER_BACK.index(block)


VMEM = pl.BlockSpec(memory_space=pltpu.VMEM)
HBM = pl.BlockSpec(memory_space=pltpu.HBM)


def lanes_of(shape):
    return lax.broadcasted_iota(jnp.int32, shape, 1)


def rows_of(shape):
    return lax.broadcasted_iota(jnp.int32, shape, 0)


def features(signal, taps):
    return (
        taps[:, 0:1] * signal
        + taps[:, 1:2] * pltpu.roll(signal, 1, 1)
        + taps[:, 2:3] * pltpu.roll(signal, 2, 1)
    )


def columns_of(rows):
    spare = 16 - sum(row.shape[0] for row in rows)
    return jnp.transpose(jnp.concatenate(list(rows) + [jnp.zeros((spare, 256), f32)], axis=0))


def spread_rows(rows):
    count = sum(row.shape[0] for row in rows)
    values = jnp.concatenate(list(rows) + [jnp.zeros((8 - count, 256), f32)], axis=0)
    terms = []
    for _ in range(3):
        terms.append(values.astype(bf16).astype(f32))
        values = values - terms[-1]
    shape = (24, LANES * count)
    pick = (rows_of(shape) % 8 == lanes_of(shape) // LANES).astype(bf16)
    columns = jnp.transpose(jnp.concatenate(terms, axis=0)).astype(bf16)
    return jnp.dot(columns, pick, preferred_element_type=f32)


STORES = 4


def message_kernel(q_hbm, k_hbm, v_hbm, taps_hbm, filt_hbm, out_hbm, qf, ql, kk, vv, taps_ref, filt_ref, wide_ref, out_ref, sems, out_sems):
    loads = [
        pltpu.make_async_copy(taps_hbm, taps_ref, sems.at[0]),
        pltpu.make_async_copy(k_hbm, kk, sems.at[1]),
        pltpu.make_async_copy(v_hbm, vv, sems.at[2]),
        pltpu.make_async_copy(filt_hbm, filt_ref, sems.at[3]),
        pltpu.make_async_copy(q_hbm.at[:, 0:LANES], qf, sems.at[4]),
        pltpu.make_async_copy(q_hbm.at[:, BLOCK - LANES:], ql, sems.at[5]),
    ]
    for copy in loads:
        copy.start()
    loads[0].wait()
    wide_ref[...] = spread_rows((taps_ref[1], taps_ref[2]))
    for copy in loads[1:]:
        copy.wait()
    lane = lanes_of((16, LANES))
    small_row = rows_of((8, LANES))
    chunks = sorted(range(PEERS // 2), key=lambda chunk: place_there(2 * chunk))
    stores = []
    for done, chunk in enumerate(chunks):
        rows = slice(16 * chunk, 16 * chunk + 16)
        key = kk[rows, :].astype(f32)
        value = vv[rows, :].astype(f32)

        def features(signal, first):
            taps = [
                jnp.concatenate([wide_ref[rows, LANES * at:LANES * (at + 1)]] * TILES, axis=1)
                for at in range(first, first + 3)
            ]
            return taps[0] * signal + taps[1] * pltpu.roll(signal, 1, 1) + taps[2] * pltpu.roll(signal, 2, 1)

        product = features(key, 0) * features(value, 3)

        def ends(first, last, place):
            return pltpu.roll(jnp.where(lane >= 64, last, first), place, 1)

        k_ends = ends(key[:, 0:LANES], key[:, BLOCK - LANES:], 2)
        v_ends = ends(value[:, 0:LANES], value[:, BLOCK - LANES:], 6)
        q_ends = ends(qf[rows, :].astype(f32), ql[rows, :].astype(f32), 10)
        wide = jnp.where(small_row < 2, filt_ref[chunk:chunk + 1, 0:LANES],
                         jnp.where(small_row < 4, filt_ref[chunk:chunk + 1, LANES:2 * LANES],
                                   jnp.where(small_row < 6, filt_ref[chunk:chunk + 1, 2 * LANES:3 * LANES],
                                             filt_ref[chunk:chunk + 1, 3 * LANES:4 * LANES])))
        lags = jnp.where(small_row % 2 == 1, wide, pltpu.roll(wide, 64, 1))
        lags = jnp.concatenate((lags, lags), axis=0)
        edge = jnp.where(lane < 4, k_ends, jnp.where(lane < 8, v_ends, jnp.where(lane < 12, q_ends, lags)))
        for half in range(2):
            place = place_there(2 * chunk + half)
            piece = slice(8 * half, 8 * half + 8)
            for tile in range(TILES):
                out_ref[place, tile] = product[piece, LANES * tile:LANES * (tile + 1)].astype(bf16)
            out_ref[place, TILES] = edge[piece].astype(bf16)
        if (done + 1) % (len(chunks) // STORES) == 0:
            span = slice(PEERS // STORES * len(stores), PEERS // STORES * (len(stores) + 1))
            stores.append(pltpu.make_async_copy(out_ref.at[span], out_hbm.at[span], out_sems.at[len(stores)]))
            stores[-1].start()
    for copy in stores:
        copy.wait()


def gate_kernel(q_ref, k_ref, v_ref, taps_ref, live_ref, gain_ref, query_ref, skip_ref, aux_ref, table_ref):
    table_ref[...] = columns_of(
        (taps_ref[0], taps_ref[1], taps_ref[2], live_ref[...].astype(f32), gain_ref[...])
    )
    own = table_ref[pl.ds(pl.multiple_of(own_group(lax.axis_index("seq")) * OWN, OWN), OWN), :]
    kind = lanes_of((OWN, LANES)) // 4
    for tap in range(3):
        aux_ref[tap] = jnp.where(
            kind == 0, own[:, 3 + tap:4 + tap], jnp.where(kind == 1, own[:, 6 + tap:7 + tap], own[:, tap:tap + 1])
        )
    for place in range(2):
        aux_ref[3 + place] = jnp.broadcast_to(own[:, 9 + place:10 + place], (OWN, LANES))
    for chunk in range(PEERS // 2):
        rows = slice(16 * chunk, 16 * chunk + 16)
        taps = table_ref[rows, :]
        feat_query = features(q_ref[rows, :].astype(f32), taps[:, 0:3])
        feat_key = features(k_ref[rows, :].astype(f32), taps[:, 3:6])
        feat_value = features(v_ref[rows, :].astype(f32), taps[:, 6:9])
        product = (feat_key * feat_value).astype(bf16).astype(f32)
        finished = lanes_of((16, BLOCK)) < 2
        query_ref[rows, :] = jnp.where(finished, 1.0, taps[:, 9:10] * feat_query)
        skip_ref[rows, :] = jnp.where(finished, 0.0, taps[:, 10:11] * product)


DEPTH = 4
STEPS = 64 // DEPTH


def conv_kernel(msg_ref, aux_ref, out_ref, lag_ref, toep_ref, rows_ref, left_ref, sum_ref):
    lane = lanes_of((256, LANES))
    pad = 8 * (DEPTH - 1)
    edge = jnp.concatenate([msg_ref[place_from(block), TILES].astype(f32) for block in range(PEERS)], axis=0)
    lag_ref[...] = jnp.where(lane < 64, pltpu.roll(edge, 64, 1), pltpu.roll(edge, 255, 0))

    earlier = jnp.concatenate((jnp.zeros((8, LANES), f32), edge[:-8]), axis=0)
    joined = jnp.where(lane % 4 < 2, earlier, edge)

    def spread(index):
        return jnp.concatenate([aux_ref[index]] * PEERS, axis=0)

    feat = (
        spread(0) * joined
        + spread(1) * pltpu.roll(joined, 1, 1)
        + spread(2) * pltpu.roll(joined, 2, 1)
    )
    first_product = pltpu.roll(feat * pltpu.roll(feat, LANES - 4, 1), LANES - 2, 1)
    first_product = first_product.astype(bf16).astype(f32)
    first_query = pltpu.roll(feat, LANES - 10, 1)

    rows_ref[0:pad, :] = jnp.zeros((pad, 256), f32)
    for peer in range(PEERS):
        for tile in range(TILES):
            part = msg_ref[place_from(peer), tile].astype(f32)
            if tile == 0:
                part = jnp.where(lane[:8] < 2, first_product[8 * peer:8 * peer + 8], part)
            start = pad + 16 * peer + 8 * (tile // 2)
            rows_ref[start:start + 8, LANES * (tile % 2):LANES * (tile % 2 + 1)] = part
    for back in range(DEPTH):
        left_ref[:, 256 * back:256 * (back + 1)] = rows_ref[pad - 8 * back:pad - 8 * back + 512, :].astype(bf16)

    lower = lanes_of((LANES, LANES)) >= rows_of((LANES, LANES))
    toep_ref[0] = jnp.zeros((LANES, LANES), bf16)
    turned = jnp.zeros((LANES, LANES), f32)
    for step in range(STEPS):
        for e in range(2 * DEPTH * step, 2 * DEPTH * (step + 1)):
            before = turned
            row = jnp.broadcast_to(lag_ref[2 * e:2 * e + 1, :], (LANES, LANES))
            turned = pltpu.roll(row, 0, 1, stride=1, stride_axis=0)
            toep_ref[e + 1] = jnp.where(lower, turned, before).astype(bf16)
        first = DEPTH * step
        parts = []
        for back in range(DEPTH):
            for half in range(2):
                at = 1 + 2 * (first + back) - half
                parts.append(jnp.concatenate((toep_ref[at], toep_ref[at + 1]), axis=1))
        right = jnp.concatenate(parts, axis=0)
        offset = 8 * first
        got = jnp.dot(left_ref[0:512 - offset, :], right, preferred_element_type=f32)
        if step == 0:
            sum_ref[...] = got
        else:
            sum_ref[offset:, :] += got

        for peer in range(DEPTH // 2 * step, DEPTH // 2 * (step + 1)):
            group = slice(8 * peer, 8 * peer + 8)
            result = sum_ref[16 * peer:16 * peer + 16, :].astype(bf16)
            head = result[0:8, 0:LANES].astype(f32)
            done = aux_ref[3] * first_query[group] * (head + aux_ref[4] * first_product[group])
            out_ref[place_back(peer), :, 0:LANES] = jnp.where(lane[:8] < 2, done, head).astype(bf16)
            out_ref[place_back(peer), :, LANES:256] = result[0:8, LANES:]
            out_ref[place_back(peer), :, 256:512] = result[8:16]


def shards(stream_q, stream_k, stream_v, short_taps, filters, live_mask, skip_gain):
    taps_wide = jnp.transpose(short_taps, (0, 2, 1))
    message = pl.pallas_call(
        message_kernel,
        out_shape=jax.ShapeDtypeStruct((PEERS, TILES + 1, 8, LANES), bf16),
        in_specs=[HBM] * 5,
        out_specs=HBM,
        scratch_shapes=[
            pltpu.VMEM((256, LANES), bf16),
            pltpu.VMEM((256, LANES), bf16),
            pltpu.VMEM((256, BLOCK), bf16),
            pltpu.VMEM((256, BLOCK), bf16),
            pltpu.VMEM((3, 3, 256), f32),
            pltpu.VMEM((16, BLOCK), f32),
            pltpu.VMEM((256, 6 * LANES), f32),
            pltpu.VMEM((PEERS, TILES + 1, 8, LANES), bf16),
            pltpu.SemaphoreType.DMA((6,)),
            pltpu.SemaphoreType.DMA((STORES,)),
        ],
        name="message",
    )(stream_q, stream_k, stream_v, taps_wide, filters)
    arrived = lax.all_to_all(message, "seq", split_axis=0, concat_axis=0, tiled=True, axis_index_groups=[ORDER_OUT])

    query, skip, aux = pl.pallas_call(
        gate_kernel,
        out_shape=[jax.ShapeDtypeStruct((256, BLOCK), f32)] * 2 + [jax.ShapeDtypeStruct((5, OWN, LANES), f32)],
        in_specs=[VMEM] * 6,
        out_specs=[VMEM] * 3,
        scratch_shapes=[pltpu.VMEM((256, 16), f32)],
        compiler_params=pltpu.CompilerParams(vmem_limit_bytes=16 << 20),
        cost_estimate=pl.CostEstimate(flops=4000000, bytes_accessed=2 << 20, transcendentals=0),
        name="gate",
    )(stream_q, stream_k, stream_v, taps_wide, live_mask[None, :], skip_gain[None, :])

    convolved = pl.pallas_call(
        conv_kernel,
        out_shape=jax.ShapeDtypeStruct((PEERS, OWN, BLOCK), bf16),
        in_specs=[VMEM] * 2,
        out_specs=VMEM,
        scratch_shapes=[
            pltpu.VMEM((256, LANES), f32),
            pltpu.VMEM((129, LANES, LANES), bf16),
            pltpu.VMEM((512 + 8 * (DEPTH - 1), 256), f32),
            pltpu.VMEM((512, 256 * DEPTH), bf16),
            pltpu.VMEM((512, 256), f32),
        ],
        compiler_params=pltpu.CompilerParams(vmem_limit_bytes=32 << 20),
        cost_estimate=pl.CostEstimate(flops=2300000000, bytes_accessed=1 << 20, transcendentals=0),
        name="conv",
    )(arrived, aux)
    back = lax.all_to_all(convolved, "seq", split_axis=0, concat_axis=0, tiled=True, axis_index_groups=[ORDER_BACK])
    return (query * (back.reshape(256, BLOCK).astype(f32) + skip)).astype(bf16)


def solution(mesh):
    in_specs = (
        P("tp", "seq"),
        P("tp", "seq"),
        P("tp", "seq"),
        P(None, "tp", None),
        P("tp", "seq"),
        P("tp"),
        P("tp"),
    )
    return jax.shard_map(shards, mesh=mesh, in_specs=in_specs, out_specs=P("tp", "seq"), check_vma=False)
```

time: 71.6 us -> 70 us (0.978)
  blocking collectives: 0 us -> 24.8 us
  waiting for transfers between devices: 30.2 us -> 17.6 us
  starting transfers between devices: 31.4 us -> 18.9 us
  Pallas kernels: 8.14 us -> 6.83 us
    all_to_all x0 -> x1, blocking collectives: none -> 24.8 us  [shards(): lax.all_to_all(convolved, 'seq', split_axis=0, concat_axis=0, tiled=True,...]
    all_to_all x1 -> x0, waiting for transfers between devices: 12.6 us -> none  [shards(): lax.all_to_all(convolved, 'seq', split_axis=0, concat_axis=0, tiled=True,...]
    all_to_all x1 -> x0, starting transfers between devices: 12.5 us -> none  [shards(): lax.all_to_all(convolved, 'seq', split_axis=0, concat_axis=0, tiled=True,...]
    pallas_call x1, Pallas kernels: 3.89 us -> 3.12 us  [shards(): pl.pallas_call(conv_kernel, out_shape=jax.ShapeDtypeStruct((PEERS, OWN, B...]
  transfers between devices with their start and end apart: 2 -> 1, of which waited for: 2 -> 1; matrix products, arithmetic and copies ran while one was open for 0% -> 0% of each run, Pallas kernels for 2% -> 2%
where the time goes in v3:
time: 70 us; the launch traced here: 69.7 us
  blocking collectives  24.8 us (35%)
  starting transfers between devices  18.9 us (27%)
  waiting for transfers between devices  17.6 us (25%)
  Pallas kernels  6.83 us (10%)
  other arithmetic  0.83 us (1%)
    all_to_all x1, blocking collectives, shards(): lax.all_to_all(convolved, 'seq', split_axis=0, concat_axis=0, tiled=True,...  24.8 us
    all_to_all x1, starting transfers between devices, shards(): lax.all_to_all(message, 'seq', split_axis=0, concat_axis=0, tiled=True, a...  18.9 us
    all_to_all x1, waiting for transfers between devices, shards(): lax.all_to_all(message, 'seq', split_axis=0, concat_axis=0, tiled=True, a...  17.6 us
    pallas_call x1, Pallas kernels, shards(): pl.pallas_call(conv_kernel, out_shape=jax.ShapeDtypeStruct((PEERS, OWN, B...  3.12 us
    pallas_call x1, Pallas kernels, shards(): pl.pallas_call(message_kernel, out_shape=jax.ShapeDtypeStruct((PEERS, TIL...  2.3 us
    pallas_call x1, Pallas kernels, shards(): pl.pallas_call(gate_kernel, out_shape=[jax.ShapeDtypeStruct((256, BLOCK),...  1.41 us
  transfers between devices with their start and end apart: 1, of which 1 were waited for; matrix products, arithmetic and copies ran while one was open for 0% of the time, Pallas kernels for 2%

profile of v3, /device:TPU:24, one launch (start us, length us, event | category | flops | bytes accessed | tf_op | source)
XLA Modules:
  0.0 69.7 jit_solution(3973739251191937254)
XLA Ops:
  0.0 0.0 copy-start.2
  0.0 2.3 %message.1 = bf16[32,5,8,128]{3,2,1,0:T(8,128)(2,1)} custom-call(bf16[256,512]{1,0:T(8,128)(2,1)} %q_hbm.1, bf16[256,512]{1,0:T(8,128)(2,1)} %k_hbm.1, bf16[256,512]{1,0:T(8,128)(2,1)} %v_hbm.1, f32[3,3,256]{2,1,0:T(4,128)} %bitcast.6, f32[16,512]{1,0:T(8,128)} %filt_hbm.1), custom_call_target="tpu_custom_call" | custom-call | tf_op jit(solution)/shard_map/message/pallas_call | solution.py:231
  2.3 0.0 copy-start
  2.3 0.0 copy-start.1
  2.3 0.0 copy-start.3
  2.3 0.0 copy-start.5
  2.4 18.9 %all-to-all-start = ((bf16[32,5,8,128]{3,2,1,0:T(8,128)(2,1)}), bf16[32,5,8,128]{3,2,1,0:T(8,128)(2,1)S(1)}, u32[]{:S(2)}, u32[]{:S(2)}) async-start(bf16[32,5,8,128]{3,2,1,0:T(8,128)(2,1)} %message.1), calls=%async_computation | async-start | bytes 655360 | tf_op jit(solution)/shard_map/all_to_all | solution.py:250
  21.3 0.0 copy-start.4
  21.3 0.0 copy-done.2
  21.3 0.0 copy-done
  21.3 0.0 copy-done.1
  21.3 0.0 copy-done.3
  21.3 0.0 copy-done.5
  21.3 0.6 copy-done.4
  22.0 1.4 %gate.1 = (f32[256,512]{1,0:T(8,128)S(1)}, f32[256,512]{1,0:T(8,128)S(1)}, f32[5,8,128]{2,1,0:T(8,128)S(1)}) custom-call(bf16[256,512]{1,0:T(8,128)(2,1)S(1)} %copy-done, bf16[256,512]{1,0:T(8,128)(2,1)S(1)} %copy-done.1, bf16[256,512]{1,0:T(8,128)(2,1)S(1)} %copy-done.2, f32[3,3,256]{2,1,0:T(4,128)S(1)} %bitcast.7, s32[1,256]{1,0:T(1,128)S(1)} %bitcast.8, ...), custom_call_target="tpu_custom_call" | custom-call | flops 4000000 | bytes 2097152 | tf_op jit(solution)/shard_map/gate/pallas_call | solution.py:252
  23.4 17.6 %all-to-all-done.msg_ref = bf16[32,5,8,128]{3,2,1,0:T(8,128)(2,1)S(1)} async-done(((bf16[32,5,8,128]{3,2,1,0:T(8,128)(2,1)}), bf16[32,5,8,128]{3,2,1,0:T(8,128)(2,1)S(1)}, u32[]{:S(2)}, u32[]{:S(2)}) %all-to-all-start) | async-done | bytes 327712 | tf_op jit(solution)/shard_map/all_to_all | solution.py:250
  40.9 3.1 %conv.1 = bf16[32,8,512]{2,1,0:T(8,128)(2,1)S(1)} custom-call(bf16[32,5,8,128]{3,2,1,0:T(8,128)(2,1)S(1)} %all-to-all-done.msg_ref, f32[5,8,128]{2,1,0:T(8,128)S(1)} %get-tuple-element.9.aux_ref), custom_call_target="tpu_custom_call" | custom-call | flops 2300000000 | bytes 1048576 | tf_op jit(solution)/shard_map/conv/pallas_call | solution.py:263
  44.1 24.8 %all_to_all.10 = bf16[32,8,512]{2,1,0:T(8,128)(2,1)S(1)} all-to-all(bf16[32,8,512]{2,1,0:T(8,128)(2,1)S(1)} %conv.1), channel_id=1, replica_groups={{256,272,288,304,320,336,352,368,384,400,416,432,448,464,480,496,0,16,3..., dimensions={0} | all-to-all | bytes 524288 | tf_op jit(solution)/shard_map/all_to_all | solution.py:279
  68.9 0.8 %fusion.1 = bf16[256,512]{1,0:T(8,128)(2,1)} fusion(f32[256,512]{1,0:T(8,128)S(1)} %get-tuple-element.8, f32[256,512]{1,0:T(8,128)S(1)} %get-tuple-element.10, bf16[32,8,512]{2,1,0:T(8,128)(2,1)S(1)} %all_to_all.10), kind=kLoop, calls=%fused_computation.2 | loop fusion | flops 524288 | bytes 1572864 | tf_op jit(solution)/shard_map/convert_element_type | solution.py:280
Async XLA Ops:
  0.0 21.3 %copy-start.2 = (bf16[256,512]{1,0:T(8,128)(2,1)S(1)}, bf16[256,512]{1,0:T(8,128)(2,1)}, u32[]{:S(2)}) copy-start(bf16[256,512]{1,0:T(8,128)(2,1)} %v_hbm.1) | copy-start | bytes 786436
  2.3 19.0 %copy-start = (bf16[256,512]{1,0:T(8,128)(2,1)S(1)}, bf16[256,512]{1,0:T(8,128)(2,1)}, u32[]{:S(2)}) copy-start(bf16[256,512]{1,0:T(8,128)(2,1)} %q_hbm.1) | copy-start | bytes 786436
  2.3 19.0 %copy-start.1 = (bf16[256,512]{1,0:T(8,128)(2,1)S(1)}, bf16[256,512]{1,0:T(8,128)(2,1)}, u32[]{:S(2)}) copy-start(bf16[256,512]{1,0:T(8,128)(2,1)} %k_hbm.1) | copy-start | bytes 786436
  2.3 19.0 %copy-start.3 = (f32[3,256,3]{1,2,0:T(4,128)S(1)}, f32[3,256,3]{1,2,0:T(4,128)}, u32[]{:S(2)}) copy-start(f32[3,256,3]{1,2,0:T(4,128)} %param.10) | copy-start | bytes 27652
  2.3 19.0 %copy-start.5 = (f32[256]{0:T(256)S(1)}, f32[256]{0:T(256)}, u32[]{:S(2)}) copy-start(f32[256]{0:T(256)} %param.13) | copy-start | bytes 3076
  2.4 38.6 %all-to-all-start = ((bf16[32,5,8,128]{3,2,1,0:T(8,128)(2,1)}), bf16[32,5,8,128]{3,2,1,0:T(8,128)(2,1)S(1)}, u32[]{:S(2)}, u32[]{:S(2)}) async-start(bf16[32,5,8,128]{3,2,1,0:T(8,128)(2,1)} %message.1), calls=%async_computation | async-start | bytes 655360 | tf_op jit(solution)/shard_map/all_to_all | solution.py:250
  21.3 0.7 copy-start.4

commit v4 on v3

--- a/solution.py
+++ b/solution.py
@@ -11,13 +11,14 @@
 BLOCK = 512
 LANES = 128
 TILES = BLOCK // LANES
-FIRST_OUT, FIRST_BACK = 22, 16
-ORDER_OUT = [(FIRST_OUT + place) % PEERS for place in range(PEERS)]
-ORDER_BACK = [(FIRST_BACK + place) % PEERS for place in range(PEERS)]
+FIRST_OUT, FIRST_BACK = 23, 17
+ORDER_OUT, ORDER_BACK = (
+    [first] + [index for index in range(PEERS) if index != first] for first in (FIRST_OUT, FIRST_BACK)
+)
 
 
 def own_group(index):
-    return lax.rem(index + PEERS - FIRST_BACK, PEERS)
+    return jnp.where(index == FIRST_BACK, 0, jnp.where(index < FIRST_BACK, index + 1, index))
 
 
 def place_there(group):
@@ -90,7 +91,8 @@
         copy.wait()
     lane = lanes_of((16, LANES))
     small_row = rows_of((8, LANES))
-    chunks = sorted(range(PEERS // 2), key=lambda chunk: place_there(2 * chunk))
+    group_at = {place_there(group): group for group in range(PEERS)}
+    chunks = list(dict.fromkeys(group_at[place] // 2 for place in range(PEERS)))
     stores = []
     for done, chunk in enumerate(chunks):
         rows = slice(16 * chunk, 16 * chunk + 16)
@@ -125,10 +127,14 @@
             for tile in range(TILES):
                 out_ref[place, tile] = product[piece, LANES * tile:LANES * (tile + 1)].astype(bf16)
             out_ref[place, TILES] = edge[piece].astype(bf16)
-        if (done + 1) % (len(chunks) // STORES) == 0:
+        full = {place_there(2 * chunk + half) for chunk in chunks[:done + 1] for half in range(2)}
+        while len(stores) < STORES:
             span = slice(PEERS // STORES * len(stores), PEERS // STORES * (len(stores) + 1))
+            if not full.issuperset(range(span.start, span.stop)):
+                break
             stores.append(pltpu.make_async_copy(out_ref.at[span], out_hbm.at[span], out_sems.at[len(stores)]))
             stores[-1].start()
+    assert len(stores) == STORES
     for copy in stores:
         copy.wait()
 

time: 70 us -> 68.3 us (0.976)
  waiting for transfers between devices: 17.6 us -> 15.4 us
    all_to_all x1, waiting for transfers between devices: 17.6 us -> 15.4 us  [shards(): lax.all_to_all(message, 'seq', split_axis=0, concat_axis=0, tiled=True, a...]
where the time goes in v4:
time: 68.3 us; the launch traced here: 67.5 us
  blocking collectives  24.8 us (36%)
  starting transfers between devices  18.9 us (28%)
  waiting for transfers between devices  15.4 us (23%)
  Pallas kernels  6.83 us (10%)
  other arithmetic  0.83 us (1%)
    all_to_all x1, blocking collectives, shards(): lax.all_to_all(convolved, 'seq', split_axis=0, concat_axis=0, tiled=True,...  24.8 us
    all_to_all x1, starting transfers between devices, shards(): lax.all_to_all(message, 'seq', split_axis=0, concat_axis=0, tiled=True, a...  18.9 us
    all_to_all x1, waiting for transfers between devices, shards(): lax.all_to_all(message, 'seq', split_axis=0, concat_axis=0, tiled=True, a...  15.4 us
    pallas_call x1, Pallas kernels, shards(): pl.pallas_call(conv_kernel, out_shape=jax.ShapeDtypeStruct((PEERS, OWN, B...  3.12 us
    pallas_call x1, Pallas kernels, shards(): pl.pallas_call(message_kernel, out_shape=jax.ShapeDtypeStruct((PEERS, TIL...  2.3 us
    pallas_call x1, Pallas kernels, shards(): pl.pallas_call(gate_kernel, out_shape=[jax.ShapeDtypeStruct((256, BLOCK),...  1.41 us
  transfers between devices with their start and end apart: 1, of which 1 were waited for; matrix products, arithmetic and copies ran while one was open for 0% of the time, Pallas kernels for 2%

profile of v4, /device:TPU:24, one launch (start us, length us, event | category | flops | bytes accessed | tf_op | source)
XLA Modules:
  0.0 67.5 jit_solution(12835872429194346469)
XLA Ops:
  0.0 0.0 copy-start.2
  0.0 2.3 %message.1 = bf16[32,5,8,128]{3,2,1,0:T(8,128)(2,1)} custom-call(bf16[256,512]{1,0:T(8,128)(2,1)} %q_hbm.1, bf16[256,512]{1,0:T(8,128)(2,1)} %k_hbm.1, bf16[256,512]{1,0:T(8,128)(2,1)} %v_hbm.1, f32[3,3,256]{2,1,0:T(4,128)} %bitcast.6, f32[16,512]{1,0:T(8,128)} %filt_hbm.1), custom_call_target="tpu_custom_call" | custom-call | tf_op jit(solution)/shard_map/message/pallas_call | solution.py:237
  2.3 0.0 copy-start
  2.3 0.0 copy-start.1
  2.3 0.0 copy-start.3
  2.3 0.0 copy-start.5
  2.4 18.9 %all-to-all-start = ((bf16[32,5,8,128]{3,2,1,0:T(8,128)(2,1)}), bf16[32,5,8,128]{3,2,1,0:T(8,128)(2,1)S(1)}, u32[]{:S(2)}, u32[]{:S(2)}) async-start(bf16[32,5,8,128]{3,2,1,0:T(8,128)(2,1)} %message.1), calls=%async_computation | async-start | bytes 655360 | tf_op jit(solution)/shard_map/all_to_all | solution.py:256
  21.3 0.0 copy-start.4
  21.3 0.0 copy-done.2
  21.3 0.0 copy-done
  21.3 0.0 copy-done.1
  21.3 0.0 copy-done.3
  21.3 0.0 copy-done.5
  21.3 0.6 copy-done.4
  21.9 1.4 %gate.1 = (f32[256,512]{1,0:T(8,128)S(1)}, f32[256,512]{1,0:T(8,128)S(1)}, f32[5,8,128]{2,1,0:T(8,128)S(1)}) custom-call(bf16[256,512]{1,0:T(8,128)(2,1)S(1)} %copy-done, bf16[256,512]{1,0:T(8,128)(2,1)S(1)} %copy-done.1, bf16[256,512]{1,0:T(8,128)(2,1)S(1)} %copy-done.2, f32[3,3,256]{2,1,0:T(4,128)S(1)} %bitcast.7, s32[1,256]{1,0:T(1,128)S(1)} %bitcast.8, ...), custom_call_target="tpu_custom_call" | custom-call | flops 4000000 | bytes 2097152 | tf_op jit(solution)/shard_map/gate/pallas_call | solution.py:258
  23.4 15.4 %all-to-all-done.msg_ref = bf16[32,5,8,128]{3,2,1,0:T(8,128)(2,1)S(1)} async-done(((bf16[32,5,8,128]{3,2,1,0:T(8,128)(2,1)}), bf16[32,5,8,128]{3,2,1,0:T(8,128)(2,1)S(1)}, u32[]{:S(2)}, u32[]{:S(2)}) %all-to-all-start) | async-done | bytes 327712 | tf_op jit(solution)/shard_map/all_to_all | solution.py:256
  38.7 3.1 %conv.1 = bf16[32,8,512]{2,1,0:T(8,128)(2,1)S(1)} custom-call(bf16[32,5,8,128]{3,2,1,0:T(8,128)(2,1)S(1)} %all-to-all-done.msg_ref, f32[5,8,128]{2,1,0:T(8,128)S(1)} %get-tuple-element.9.aux_ref), custom_call_target="tpu_custom_call" | custom-call | flops 2300000000 | bytes 1048576 | tf_op jit(solution)/shard_map/conv/pallas_call | solution.py:269
  41.9 24.8 %all_to_all.10 = bf16[32,8,512]{2,1,0:T(8,128)(2,1)S(1)} all-to-all(bf16[32,8,512]{2,1,0:T(8,128)(2,1)S(1)} %conv.1), channel_id=1, replica_groups={{272,0,16,32,48,64,80,96,112,128,144,160,176,192,208,224,240,256,288,30..., dimensions={0} | all-to-all | bytes 524288 | tf_op jit(solution)/shard_map/all_to_all | solution.py:285
  66.7 0.8 %fusion.1 = bf16[256,512]{1,0:T(8,128)(2,1)} fusion(f32[256,512]{1,0:T(8,128)S(1)} %get-tuple-element.8, f32[256,512]{1,0:T(8,128)S(1)} %get-tuple-element.10, bf16[32,8,512]{2,1,0:T(8,128)(2,1)S(1)} %all_to_all.10), kind=kLoop, calls=%fused_computation.2 | loop fusion | flops 524288 | bytes 1572864 | tf_op jit(solution)/shard_map/convert_element_type | solution.py:286
Async XLA Ops:
  0.0 21.3 %copy-start.2 = (bf16[256,512]{1,0:T(8,128)(2,1)S(1)}, bf16[256,512]{1,0:T(8,128)(2,1)}, u32[]{:S(2)}) copy-start(bf16[256,512]{1,0:T(8,128)(2,1)} %v_hbm.1) | copy-start | bytes 786436
  2.3 19.0 %copy-start = (bf16[256,512]{1,0:T(8,128)(2,1)S(1)}, bf16[256,512]{1,0:T(8,128)(2,1)}, u32[]{:S(2)}) copy-start(bf16[256,512]{1,0:T(8,128)(2,1)} %q_hbm.1) | copy-start | bytes 786436
  2.3 19.0 %copy-start.1 = (bf16[256,512]{1,0:T(8,128)(2,1)S(1)}, bf16[256,512]{1,0:T(8,128)(2,1)}, u32[]{:S(2)}) copy-start(bf16[256,512]{1,0:T(8,128)(2,1)} %k_hbm.1) | copy-start | bytes 786436
  2.3 19.0 %copy-start.3 = (f32[3,256,3]{1,2,0:T(4,128)S(1)}, f32[3,256,3]{1,2,0:T(4,128)}, u32[]{:S(2)}) copy-start(f32[3,256,3]{1,2,0:T(4,128)} %param.10) | copy-start | bytes 27652
  2.3 19.0 %copy-start.5 = (f32[256]{0:T(256)S(1)}, f32[256]{0:T(256)}, u32[]{:S(2)}) copy-start(f32[256]{0:T(256)} %param.13) | copy-start | bytes 3076
  2.4 36.4 %all-to-all-start = ((bf16[32,5,8,128]{3,2,1,0:T(8,128)(2,1)}), bf16[32,5,8,128]{3,2,1,0:T(8,128)(2,1)S(1)}, u32[]{:S(2)}, u32[]{:S(2)}) async-start(bf16[32,5,8,128]{3,2,1,0:T(8,128)(2,1)} %message.1), calls=%async_computation | async-start | bytes 655360 | tf_op jit(solution)/shard_map/all_to_all | solution.py:256
  21.3 0.7 %copy-start.4 = (s32[256]{0:T(256)S(1)}, s32[256]{0:T(256)}, u32[]{:S(2)}) copy-start(s32[256]{0:T(256)} %param.12) | copy-start | bytes 3076

commit v5 on v4

--- a/solution.py
+++ b/solution.py
@@ -12,13 +12,15 @@
 LANES = 128
 TILES = BLOCK // LANES
 FIRST_OUT, FIRST_BACK = 23, 17
-ORDER_OUT, ORDER_BACK = (
-    [first] + [index for index in range(PEERS) if index != first] for first in (FIRST_OUT, FIRST_BACK)
-)
+IN_TURN = [index for step in range(PEERS // 2) for index in (step, step + PEERS // 2)]
+ORDER_OUT = [FIRST_OUT] + [index for index in range(PEERS) if index != FIRST_OUT]
+ORDER_BACK = [FIRST_BACK] + [index for index in IN_TURN if index != FIRST_BACK]
 
 
 def own_group(index):
-    return jnp.where(index == FIRST_BACK, 0, jnp.where(index < FIRST_BACK, index + 1, index))
+    half = PEERS // 2
+    turn = 2 * lax.rem(index, half) + index // half
+    return jnp.where(index == FIRST_BACK, 0, jnp.where(turn < IN_TURN.index(FIRST_BACK), turn + 1, turn))
 
 
 def place_there(group):
@@ -163,6 +165,20 @@
         skip_ref[rows, :] = jnp.where(finished, 0.0, taps[:, 10:11] * product)
 
 
+def final_kernel(back_ref, query_ref, skip_ref, out_hbm, out_ref, sems):
+    parts = sems.shape[0]
+    copies = []
+    for part in range(parts):
+        groups = slice(PEERS // parts * part, PEERS // parts * (part + 1))
+        rows = slice(OWN * groups.start, OWN * groups.stop)
+        back = back_ref[groups].astype(f32).reshape(OWN * PEERS // parts, BLOCK)
+        out_ref[rows, :] = (query_ref[rows, :] * (back + skip_ref[rows, :])).astype(bf16)
+        copies.append(pltpu.make_async_copy(out_ref.at[rows], out_hbm.at[rows], sems.at[part]))
+        copies[-1].start()
+    for copy in copies:
+        copy.wait()
+
+
 DEPTH = 4
 STEPS = 64 // DEPTH
 
@@ -283,7 +299,15 @@
         name="conv",
     )(arrived, aux)
     back = lax.all_to_all(convolved, "seq", split_axis=0, concat_axis=0, tiled=True, axis_index_groups=[ORDER_BACK])
-    return (query * (back.reshape(256, BLOCK).astype(f32) + skip)).astype(bf16)
+    return pl.pallas_call(
+        final_kernel,
+        out_shape=jax.ShapeDtypeStruct((256, BLOCK), bf16),
+        in_specs=[VMEM] * 3,
+        out_specs=HBM,
+        scratch_shapes=[pltpu.VMEM((256, BLOCK), bf16), pltpu.SemaphoreType.DMA((4,))],
+        compiler_params=pltpu.CompilerParams(vmem_limit_bytes=16 << 20),
+        name="final",
+    )(back, query, skip)
 
 
 def solution(mesh):

time: 68.3 us -> 67.9 us (level)
  other arithmetic: 0.83 us -> 0 us
  Pallas kernels: 6.83 us -> 7.62 us
    convert_element_type x1 -> x0, other arithmetic: 0.83 us -> none  [shards(): return (query * (back.reshape(256, BLOCK).astype(f32) + skip)).astype(bf16)]
    pallas_call x0 -> x1, Pallas kernels: none -> 0.75 us  [shards(): pl.pallas_call(final_kernel, out_shape=jax.ShapeDtypeStruct((256, BLOCK),...]
where the time goes in v5:
time: 67.9 us; the launch traced here: 67.6 us
  blocking collectives  24.9 us (37%)
  starting transfers between devices  18.9 us (28%)
  waiting for transfers between devices  15.4 us (23%)
  Pallas kernels  7.62 us (11%)
    all_to_all x1, blocking collectives, shards(): lax.all_to_all(convolved, 'seq', split_axis=0, concat_axis=0, tiled=True,...  24.9 us
    all_to_all x1, starting transfers between devices, shards(): lax.all_to_all(message, 'seq', split_axis=0, concat_axis=0, tiled=True, a...  18.9 us
    all_to_all x1, waiting for transfers between devices, shards(): lax.all_to_all(message, 'seq', split_axis=0, concat_axis=0, tiled=True, a...  15.4 us
    pallas_call x1, Pallas kernels, shards(): pl.pallas_call(conv_kernel, out_shape=jax.ShapeDtypeStruct((PEERS, OWN, B...  3.12 us
    pallas_call x1, Pallas kernels, shards(): pl.pallas_call(message_kernel, out_shape=jax.ShapeDtypeStruct((PEERS, TIL...  2.34 us
    pallas_call x1, Pallas kernels, shards(): pl.pallas_call(gate_kernel, out_shape=[jax.ShapeDtypeStruct((256, BLOCK),...  1.41 us
  transfers between devices with their start and end apart: 1, of which 1 were waited for; matrix products, arithmetic and copies ran while one was open for 0% of the time, Pallas kernels for 2%

profile of v5, /device:TPU:24, one launch (start us, length us, event | category | flops | bytes accessed | tf_op | source)
XLA Modules:
  0.0 67.6 jit_solution(12301117562413455249)
XLA Ops:
  0.0 0.0 copy-start.2
  0.0 2.3 %message.1 = bf16[32,5,8,128]{3,2,1,0:T(8,128)(2,1)} custom-call(bf16[256,512]{1,0:T(8,128)(2,1)} %q_ref.1, bf16[256,512]{1,0:T(8,128)(2,1)} %k_ref.1, bf16[256,512]{1,0:T(8,128)(2,1)} %v_ref.1, f32[3,3,256]{2,1,0:T(4,128)} %bitcast.3, f32[16,512]{1,0:T(8,128)} %filt_hbm.1), custom_call_target="tpu_custom_call" | custom-call | tf_op jit(solution)/shard_map/message/pallas_call | solution.py:253
  2.4 0.0 copy-start
  2.4 0.0 copy-start.1
  2.4 0.0 copy-start.3
  2.4 0.0 copy-start.5
  2.4 18.9 %all-to-all-start = ((bf16[32,5,8,128]{3,2,1,0:T(8,128)(2,1)}), bf16[32,5,8,128]{3,2,1,0:T(8,128)(2,1)S(1)}, u32[]{:S(2)}, u32[]{:S(2)}) async-start(bf16[32,5,8,128]{3,2,1,0:T(8,128)(2,1)} %message.1), calls=%async_computation | async-start | bytes 655360 | tf_op jit(solution)/shard_map/all_to_all | solution.py:272
  21.3 0.0 copy-start.4
  21.3 0.0 copy-done.2
  21.3 0.0 copy-done
  21.3 0.0 copy-done.1
  21.3 0.0 copy-done.3
  21.4 0.0 copy-done.5
  21.4 0.6 copy-done.4
  22.0 1.4 %gate.1 = (f32[256,512]{1,0:T(8,128)S(1)}, f32[256,512]{1,0:T(8,128)S(1)}, f32[5,8,128]{2,1,0:T(8,128)S(1)}) custom-call(bf16[256,512]{1,0:T(8,128)(2,1)S(1)} %copy-done, bf16[256,512]{1,0:T(8,128)(2,1)S(1)} %copy-done.1, bf16[256,512]{1,0:T(8,128)(2,1)S(1)} %copy-done.2, f32[3,3,256]{2,1,0:T(4,128)S(1)} %bitcast.4, s32[1,256]{1,0:T(1,128)S(1)} %bitcast.5, ...), custom_call_target="tpu_custom_call" | custom-call | flops 4000000 | bytes 2097152 | tf_op jit(solution)/shard_map/gate/pallas_call | solution.py:274
  23.4 15.4 %all-to-all-done.msg_ref = bf16[32,5,8,128]{3,2,1,0:T(8,128)(2,1)S(1)} async-done(((bf16[32,5,8,128]{3,2,1,0:T(8,128)(2,1)}), bf16[32,5,8,128]{3,2,1,0:T(8,128)(2,1)S(1)}, u32[]{:S(2)}, u32[]{:S(2)}) %all-to-all-start) | async-done | bytes 327712 | tf_op jit(solution)/shard_map/all_to_all | solution.py:272
  38.8 3.1 %conv.1 = bf16[32,8,512]{2,1,0:T(8,128)(2,1)S(1)} custom-call(bf16[32,5,8,128]{3,2,1,0:T(8,128)(2,1)S(1)} %all-to-all-done.msg_ref, f32[5,8,128]{2,1,0:T(8,128)S(1)} %get-tuple-element.8.aux_ref), custom_call_target="tpu_custom_call" | custom-call | flops 2300000000 | bytes 1048576 | tf_op jit(solution)/shard_map/conv/pallas_call | solution.py:285
  41.9 24.9 %all_to_all.10.back_ref = bf16[32,8,512]{2,1,0:T(8,128)(2,1)S(1)} all-to-all(bf16[32,8,512]{2,1,0:T(8,128)(2,1)S(1)} %conv.1), channel_id=1, replica_groups={{272,0,256,16,32,288,48,304,64,320,80,336,96,352,112,368,128,384,144,40..., dimensions={0} | all-to-all | bytes 524288 | tf_op jit(solution)/shard_map/all_to_all | solution.py:301
  66.9 0.7 %final.1 = bf16[256,512]{1,0:T(8,128)(2,1)} custom-call(bf16[32,8,512]{2,1,0:T(8,128)(2,1)S(1)} %all_to_all.10.back_ref, f32[256,512]{1,0:T(8,128)S(1)} %get-tuple-element.9.query_ref, f32[256,512]{1,0:T(8,128)S(1)} %get-tuple-element.10.skip_ref), custom_call_target="tpu_custom_call" | custom-call | tf_op jit(solution)/shard_map/final/pallas_call | solution.py:302
Async XLA Ops:
  0.0 21.3 %copy-start.2 = (bf16[256,512]{1,0:T(8,128)(2,1)S(1)}, bf16[256,512]{1,0:T(8,128)(2,1)}, u32[]{:S(2)}) copy-start(bf16[256,512]{1,0:T(8,128)(2,1)} %v_ref.1) | copy-start | bytes 786436
  2.4 19.0 %copy-start = (bf16[256,512]{1,0:T(8,128)(2,1)S(1)}, bf16[256,512]{1,0:T(8,128)(2,1)}, u32[]{:S(2)}) copy-start(bf16[256,512]{1,0:T(8,128)(2,1)} %q_ref.1) | copy-start | bytes 786436
  2.4 19.0 %copy-start.1 = (bf16[256,512]{1,0:T(8,128)(2,1)S(1)}, bf16[256,512]{1,0:T(8,128)(2,1)}, u32[]{:S(2)}) copy-start(bf16[256,512]{1,0:T(8,128)(2,1)} %k_ref.1) | copy-start | bytes 786436
  2.4 19.0 %copy-start.3 = (f32[3,256,3]{1,2,0:T(4,128)S(1)}, f32[3,256,3]{1,2,0:T(4,128)}, u32[]{:S(2)}) copy-start(f32[3,256,3]{1,2,0:T(4,128)} %param.10) | copy-start | bytes 27652
  2.4 19.0 %copy-start.5 = (f32[256]{0:T(256)S(1)}, f32[256]{0:T(256)}, u32[]{:S(2)}) copy-start(f32[256]{0:T(256)} %param.13) | copy-start | bytes 3076
  2.4 36.4 %all-to-all-start = ((bf16[32,5,8,128]{3,2,1,0:T(8,128)(2,1)}), bf16[32,5,8,128]{3,2,1,0:T(8,128)(2,1)S(1)}, u32[]{:S(2)}, u32[]{:S(2)}) async-start(bf16[32,5,8,128]{3,2,1,0:T(8,128)(2,1)} %message.1), calls=%async_computation | async-start | bytes 655360 | tf_op jit(solution)/shard_map/all_to_all | solution.py:272
  21.3 0.7 %copy-start.4 = (s32[256]{0:T(256)S(1)}, s32[256]{0:T(256)}, u32[]{:S(2)}) copy-start(s32[256]{0:T(256)} %param.12) | copy-start | bytes 3076

commit v6 on v5

--- a/solution.py
+++ b/solution.py
@@ -11,9 +11,12 @@
 BLOCK = 512
 LANES = 128
 TILES = BLOCK // LANES
-FIRST_OUT, FIRST_BACK = 23, 17
+FIRST_BACK = 17
 IN_TURN = [index for step in range(PEERS // 2) for index in (step, step + PEERS // 2)]
-ORDER_OUT = [FIRST_OUT] + [index for index in range(PEERS) if index != FIRST_OUT]
+ORDER_OUT = [
+    23, 26, 17, 11, 10, 28, 1, 5, 4, 7, 16, 9, 19, 30, 13, 22,
+    0, 21, 29, 6, 12, 20, 14, 15, 3, 31, 2, 24, 25, 27, 18, 8,
+]
 ORDER_BACK = [FIRST_BACK] + [index for index in IN_TURN if index != FIRST_BACK]
 
 
@@ -181,6 +184,7 @@
 
 DEPTH = 4
 STEPS = 64 // DEPTH
+TAIL = 12
 
 
 def conv_kernel(msg_ref, aux_ref, out_ref, lag_ref, toep_ref, rows_ref, left_ref, sum_ref):
@@ -224,21 +228,29 @@
             row = jnp.broadcast_to(lag_ref[2 * e:2 * e + 1, :], (LANES, LANES))
             turned = pltpu.roll(row, 0, 1, stride=1, stride_axis=0)
             toep_ref[e + 1] = jnp.where(lower, turned, before).astype(bf16)
-        first = DEPTH * step
-        parts = []
-        for back in range(DEPTH):
-            for half in range(2):
-                at = 1 + 2 * (first + back) - half
-                parts.append(jnp.concatenate((toep_ref[at], toep_ref[at + 1]), axis=1))
+        if TAIL <= step < STEPS - 1:
+            continue
+        head = TAIL if step == STEPS - 1 else step
+        offset = 8 * DEPTH * head
+        lefts, parts = [], []
+        for part in range(head, step + 1):
+            gap = 8 * DEPTH * (part - head)
+            left = left_ref[0:512 - offset - gap, :]
+            if gap:
+                left = jnp.concatenate((jnp.zeros((gap, 256 * DEPTH), bf16), left), axis=0)
+            lefts.append(left)
+            for back in range(DEPTH):
+                for half in range(2):
+                    at = 1 + 2 * (DEPTH * part + back) - half
+                    parts.append(jnp.concatenate((toep_ref[at], toep_ref[at + 1]), axis=1))
         right = jnp.concatenate(parts, axis=0)
-        offset = 8 * first
-        got = jnp.dot(left_ref[0:512 - offset, :], right, preferred_element_type=f32)
+        got = jnp.dot(jnp.concatenate(lefts, axis=1), right, preferred_element_type=f32)
         if step == 0:
             sum_ref[...] = got
         else:
             sum_ref[offset:, :] += got
 
-        for peer in range(DEPTH // 2 * step, DEPTH // 2 * (step + 1)):
+        for peer in range(DEPTH // 2 * head, DEPTH // 2 * (step + 1)):
             group = slice(8 * peer, 8 * peer + 8)
             result = sum_ref[16 * peer:16 * peer + 16, :].astype(bf16)
             head = result[0:8, 0:LANES].astype(f32)

time: 67.9 us -> 67.8 us (level)
  waiting for transfers between devices: 15.4 us -> 13.4 us
  blocking collectives: 24.9 us -> 26.8 us
    all_to_all x1, waiting for transfers between devices: 15.4 us -> 13.4 us  [shards(): lax.all_to_all(message, 'seq', split_axis=0, concat_axis=0, tiled=True, a...]
    all_to_all x1, blocking collectives: 24.9 us -> 26.8 us  [shards(): lax.all_to_all(convolved, 'seq', split_axis=0, concat_axis=0, tiled=True,...]
where the time goes in v6:
time: 67.8 us; the launch traced here: 67.4 us
  blocking collectives  26.8 us (40%)
  starting transfers between devices  18.9 us (28%)
  waiting for transfers between devices  13.4 us (20%)
  Pallas kernels  7.51 us (11%)
    all_to_all x1, blocking collectives, shards(): lax.all_to_all(convolved, 'seq', split_axis=0, concat_axis=0, tiled=True,...  26.8 us
    all_to_all x1, starting transfers between devices, shards(): lax.all_to_all(message, 'seq', split_axis=0, concat_axis=0, tiled=True, a...  18.9 us
    all_to_all x1, waiting for transfers between devices, shards(): lax.all_to_all(message, 'seq', split_axis=0, concat_axis=0, tiled=True, a...  13.4 us
    pallas_call x1, Pallas kernels, shards(): pl.pallas_call(conv_kernel, out_shape=jax.ShapeDtypeStruct((PEERS, OWN, B...  3.06 us
    pallas_call x1, Pallas kernels, shards(): pl.pallas_call(message_kernel, out_shape=jax.ShapeDtypeStruct((PEERS, TIL...  2.3 us
    pallas_call x1, Pallas kernels, shards(): pl.pallas_call(gate_kernel, out_shape=[jax.ShapeDtypeStruct((256, BLOCK),...  1.41 us
  transfers between devices with their start and end apart: 1, of which 1 were waited for; matrix products, arithmetic and copies ran while one was open for 0% of the time, Pallas kernels for 2%

profile of v6, /device:TPU:24, one launch (start us, length us, event | category | flops | bytes accessed | tf_op | source)
XLA Modules:
  0.0 67.4 jit_solution(8246718360269009860)
XLA Ops:
  0.0 0.0 copy-start.2
  0.0 2.3 %message.1 = bf16[32,5,8,128]{3,2,1,0:T(8,128)(2,1)} custom-call(bf16[256,512]{1,0:T(8,128)(2,1)} %q_ref.1, bf16[256,512]{1,0:T(8,128)(2,1)} %k_ref.1, bf16[256,512]{1,0:T(8,128)(2,1)} %v_ref.1, f32[3,3,256]{2,1,0:T(4,128)} %bitcast.3, f32[16,512]{1,0:T(8,128)} %filt_hbm.1), custom_call_target="tpu_custom_call" | custom-call | tf_op jit(solution)/shard_map/message/pallas_call | solution.py:265
  2.3 0.0 copy-start
  2.3 0.0 copy-start.1
  2.3 0.0 copy-start.3
  2.4 0.0 copy-start.5
  2.4 18.9 %all-to-all-start = ((bf16[32,5,8,128]{3,2,1,0:T(8,128)(2,1)}), bf16[32,5,8,128]{3,2,1,0:T(8,128)(2,1)S(1)}, u32[]{:S(2)}, u32[]{:S(2)}) async-start(bf16[32,5,8,128]{3,2,1,0:T(8,128)(2,1)} %message.1), calls=%async_computation | async-start | bytes 655360 | tf_op jit(solution)/shard_map/all_to_all | solution.py:284
  21.3 0.0 copy-start.4
  21.3 0.0 copy-done.2
  21.3 0.0 copy-done
  21.3 0.0 copy-done.1
  21.3 0.0 copy-done.3
  21.3 0.0 copy-done.5
  21.3 0.6 copy-done.4
  22.0 1.4 %gate.1 = (f32[256,512]{1,0:T(8,128)S(1)}, f32[256,512]{1,0:T(8,128)S(1)}, f32[5,8,128]{2,1,0:T(8,128)S(1)}) custom-call(bf16[256,512]{1,0:T(8,128)(2,1)S(1)} %copy-done, bf16[256,512]{1,0:T(8,128)(2,1)S(1)} %copy-done.1, bf16[256,512]{1,0:T(8,128)(2,1)S(1)} %copy-done.2, f32[3,3,256]{2,1,0:T(4,128)S(1)} %bitcast.4, s32[1,256]{1,0:T(1,128)S(1)} %bitcast.5, ...), custom_call_target="tpu_custom_call" | custom-call | flops 4000000 | bytes 2097152 | tf_op jit(solution)/shard_map/gate/pallas_call | solution.py:286
  23.4 13.4 %all-to-all-done.msg_ref = bf16[32,5,8,128]{3,2,1,0:T(8,128)(2,1)S(1)} async-done(((bf16[32,5,8,128]{3,2,1,0:T(8,128)(2,1)}), bf16[32,5,8,128]{3,2,1,0:T(8,128)(2,1)S(1)}, u32[]{:S(2)}, u32[]{:S(2)}) %all-to-all-start) | async-done | bytes 327712 | tf_op jit(solution)/shard_map/all_to_all | solution.py:284
  36.8 3.1 %conv.1 = bf16[32,8,512]{2,1,0:T(8,128)(2,1)S(1)} custom-call(bf16[32,5,8,128]{3,2,1,0:T(8,128)(2,1)S(1)} %all-to-all-done.msg_ref, f32[5,8,128]{2,1,0:T(8,128)S(1)} %get-tuple-element.8.aux_ref), custom_call_target="tpu_custom_call" | custom-call | flops 2300000000 | bytes 1048576 | tf_op jit(solution)/shard_map/conv/pallas_call | solution.py:297
  39.9 26.8 %all_to_all.10.back_ref = bf16[32,8,512]{2,1,0:T(8,128)(2,1)S(1)} all-to-all(bf16[32,8,512]{2,1,0:T(8,128)(2,1)S(1)} %conv.1), channel_id=1, replica_groups={{272,0,256,16,32,288,48,304,64,320,80,336,96,352,112,368,128,384,144,40..., dimensions={0} | all-to-all | bytes 524288 | tf_op jit(solution)/shard_map/all_to_all | solution.py:313
  66.7 0.7 %final.1 = bf16[256,512]{1,0:T(8,128)(2,1)} custom-call(bf16[32,8,512]{2,1,0:T(8,128)(2,1)S(1)} %all_to_all.10.back_ref, f32[256,512]{1,0:T(8,128)S(1)} %get-tuple-element.9.query_ref, f32[256,512]{1,0:T(8,128)S(1)} %get-tuple-element.10.skip_ref), custom_call_target="tpu_custom_call" | custom-call | tf_op jit(solution)/shard_map/final/pallas_call | solution.py:314
Async XLA Ops:
  0.0 21.3 %copy-start.2 = (bf16[256,512]{1,0:T(8,128)(2,1)S(1)}, bf16[256,512]{1,0:T(8,128)(2,1)}, u32[]{:S(2)}) copy-start(bf16[256,512]{1,0:T(8,128)(2,1)} %v_ref.1) | copy-start | bytes 786436
  2.3 19.0 %copy-start = (bf16[256,512]{1,0:T(8,128)(2,1)S(1)}, bf16[256,512]{1,0:T(8,128)(2,1)}, u32[]{:S(2)}) copy-start(bf16[256,512]{1,0:T(8,128)(2,1)} %q_ref.1) | copy-start | bytes 786436
  2.3 19.0 %copy-start.1 = (bf16[256,512]{1,0:T(8,128)(2,1)S(1)}, bf16[256,512]{1,0:T(8,128)(2,1)}, u32[]{:S(2)}) copy-start(bf16[256,512]{1,0:T(8,128)(2,1)} %k_ref.1) | copy-start | bytes 786436
  2.3 19.0 %copy-start.3 = (f32[3,256,3]{1,2,0:T(4,128)S(1)}, f32[3,256,3]{1,2,0:T(4,128)}, u32[]{:S(2)}) copy-start(f32[3,256,3]{1,2,0:T(4,128)} %param.10) | copy-start | bytes 27652
  2.4 19.0 %copy-start.5 = (f32[256]{0:T(256)S(1)}, f32[256]{0:T(256)}, u32[]{:S(2)}) copy-start(f32[256]{0:T(256)} %param.13) | copy-start | bytes 3076
  2.4 34.4 %all-to-all-start = ((bf16[32,5,8,128]{3,2,1,0:T(8,128)(2,1)}), bf16[32,5,8,128]{3,2,1,0:T(8,128)(2,1)S(1)}, u32[]{:S(2)}, u32[]{:S(2)}) async-start(bf16[32,5,8,128]{3,2,1,0:T(8,128)(2,1)} %message.1), calls=%async_computation | async-start | bytes 655360 | tf_op jit(solution)/shard_map/all_to_all | solution.py:284
  21.3 0.7 %copy-start.4 = (s32[256]{0:T(256)S(1)}, s32[256]{0:T(256)}, u32[]{:S(2)}) copy-start(s32[256]{0:T(256)} %param.12) | copy-start | bytes 3076

commit v7 on v6

--- a/solution.py
+++ b/solution.py
@@ -216,8 +216,9 @@
                 part = jnp.where(lane[:8] < 2, first_product[8 * peer:8 * peer + 8], part)
             start = pad + 16 * peer + 8 * (tile // 2)
             rows_ref[start:start + 8, LANES * (tile % 2):LANES * (tile % 2 + 1)] = part
-    for back in range(DEPTH):
-        left_ref[:, 256 * back:256 * (back + 1)] = rows_ref[pad - 8 * back:pad - 8 * back + 512, :].astype(bf16)
+    left_ref[0:16, :] = jnp.zeros((16, 512), bf16)
+    for back in range(2):
+        left_ref[16:, 256 * back:256 * (back + 1)] = rows_ref[pad - 8 * back:pad - 8 * back + 512, :].astype(bf16)
 
     lower = lanes_of((LANES, LANES)) >= rows_of((LANES, LANES))
     toep_ref[0] = jnp.zeros((LANES, LANES), bf16)
@@ -235,7 +236,8 @@
         lefts, parts = [], []
         for part in range(head, step + 1):
             gap = 8 * DEPTH * (part - head)
-            left = left_ref[0:512 - offset - gap, :]
+            count = 512 - offset - gap
+            left = jnp.concatenate((left_ref[16:16 + count, :], left_ref[0:count, :]), axis=1)
             if gap:
                 left = jnp.concatenate((jnp.zeros((gap, 256 * DEPTH), bf16), left), axis=0)
             lefts.append(left)
@@ -303,7 +305,7 @@
             pltpu.VMEM((256, LANES), f32),
             pltpu.VMEM((129, LANES, LANES), bf16),
             pltpu.VMEM((512 + 8 * (DEPTH - 1), 256), f32),
-            pltpu.VMEM((512, 256 * DEPTH), bf16),
+            pltpu.VMEM((528, 512), bf16),
             pltpu.VMEM((512, 256), f32),
         ],
         compiler_params=pltpu.CompilerParams(vmem_limit_bytes=32 << 20),

time: 67.8 us -> 67.8 us (level)
  no operation moved by 1% of the time
where the time goes in v7:
time: 67.8 us; the launch traced here: 67.4 us
  blocking collectives  26.8 us (40%)
  starting transfers between devices  18.9 us (28%)
  waiting for transfers between devices  13.4 us (20%)
  Pallas kernels  7.52 us (11%)
    all_to_all x1, blocking collectives, shards(): lax.all_to_all(convolved, 'seq', split_axis=0, concat_axis=0, tiled=True,...  26.8 us
    all_to_all x1, starting transfers between devices, shards(): lax.all_to_all(message, 'seq', split_axis=0, concat_axis=0, tiled=True, a...  18.9 us
    all_to_all x1, waiting for transfers between devices, shards(): lax.all_to_all(message, 'seq', split_axis=0, concat_axis=0, tiled=True, a...  13.4 us
    pallas_call x1, Pallas kernels, shards(): pl.pallas_call(conv_kernel, out_shape=jax.ShapeDtypeStruct((PEERS, OWN, B...  3.06 us
    pallas_call x1, Pallas kernels, shards(): pl.pallas_call(message_kernel, out_shape=jax.ShapeDtypeStruct((PEERS, TIL...  2.3 us
    pallas_call x1, Pallas kernels, shards(): pl.pallas_call(gate_kernel, out_shape=[jax.ShapeDtypeStruct((256, BLOCK),...  1.41 us
  transfers between devices with their start and end apart: 1, of which 1 were waited for; matrix products, arithmetic and copies ran while one was open for 0% of the time, Pallas kernels for 2%

profile of v7, /device:TPU:24, one launch (start us, length us, event | category | flops | bytes accessed | tf_op | source)
XLA Modules:
  0.0 67.4 jit_solution(9435164570579570347)
XLA Ops:
  0.0 0.0 copy-start.2
  0.0 2.3 %message.1 = bf16[32,5,8,128]{3,2,1,0:T(8,128)(2,1)} custom-call(bf16[256,512]{1,0:T(8,128)(2,1)} %q_ref.1, bf16[256,512]{1,0:T(8,128)(2,1)} %k_ref.1, bf16[256,512]{1,0:T(8,128)(2,1)} %v_ref.1, f32[3,3,256]{2,1,0:T(4,128)} %bitcast.3, f32[16,512]{1,0:T(8,128)} %filt_hbm.1), custom_call_target="tpu_custom_call" | custom-call | tf_op jit(solution)/shard_map/message/pallas_call | solution.py:267
  2.3 0.0 copy-start
  2.3 0.0 copy-start.1
  2.3 0.0 copy-start.3
  2.4 0.0 copy-start.5
  2.4 18.9 %all-to-all-start = ((bf16[32,5,8,128]{3,2,1,0:T(8,128)(2,1)}), bf16[32,5,8,128]{3,2,1,0:T(8,128)(2,1)S(1)}, u32[]{:S(2)}, u32[]{:S(2)}) async-start(bf16[32,5,8,128]{3,2,1,0:T(8,128)(2,1)} %message.1), calls=%async_computation | async-start | bytes 655360 | tf_op jit(solution)/shard_map/all_to_all | solution.py:286
  21.3 0.0 copy-start.4
  21.3 0.0 copy-done.2
  21.3 0.0 copy-done
  21.3 0.0 copy-done.1
  21.3 0.0 copy-done.3
  21.3 0.0 copy-done.5
  21.3 0.6 copy-done.4
  22.0 1.4 %gate.1 = (f32[256,512]{1,0:T(8,128)S(1)}, f32[256,512]{1,0:T(8,128)S(1)}, f32[5,8,128]{2,1,0:T(8,128)S(1)}) custom-call(bf16[256,512]{1,0:T(8,128)(2,1)S(1)} %copy-done, bf16[256,512]{1,0:T(8,128)(2,1)S(1)} %copy-done.1, bf16[256,512]{1,0:T(8,128)(2,1)S(1)} %copy-done.2, f32[3,3,256]{2,1,0:T(4,128)S(1)} %bitcast.4, s32[1,256]{1,0:T(1,128)S(1)} %bitcast.5, ...), custom_call_target="tpu_custom_call" | custom-call | flops 4000000 | bytes 2097152 | tf_op jit(solution)/shard_map/gate/pallas_call | solution.py:288
  23.4 13.4 %all-to-all-done.msg_ref = bf16[32,5,8,128]{3,2,1,0:T(8,128)(2,1)S(1)} async-done(((bf16[32,5,8,128]{3,2,1,0:T(8,128)(2,1)}), bf16[32,5,8,128]{3,2,1,0:T(8,128)(2,1)S(1)}, u32[]{:S(2)}, u32[]{:S(2)}) %all-to-all-start) | async-done | bytes 327712 | tf_op jit(solution)/shard_map/all_to_all | solution.py:286
  36.8 3.1 %conv.1 = bf16[32,8,512]{2,1,0:T(8,128)(2,1)S(1)} custom-call(bf16[32,5,8,128]{3,2,1,0:T(8,128)(2,1)S(1)} %all-to-all-done.msg_ref, f32[5,8,128]{2,1,0:T(8,128)S(1)} %get-tuple-element.8.aux_ref), custom_call_target="tpu_custom_call" | custom-call | flops 2300000000 | bytes 1048576 | tf_op jit(solution)/shard_map/conv/pallas_call | solution.py:299
  39.9 26.8 %all_to_all.10.back_ref = bf16[32,8,512]{2,1,0:T(8,128)(2,1)S(1)} all-to-all(bf16[32,8,512]{2,1,0:T(8,128)(2,1)S(1)} %conv.1), channel_id=1, replica_groups={{272,0,256,16,32,288,48,304,64,320,80,336,96,352,112,368,128,384,144,40..., dimensions={0} | all-to-all | bytes 524288 | tf_op jit(solution)/shard_map/all_to_all | solution.py:315
  66.7 0.7 %final.1 = bf16[256,512]{1,0:T(8,128)(2,1)} custom-call(bf16[32,8,512]{2,1,0:T(8,128)(2,1)S(1)} %all_to_all.10.back_ref, f32[256,512]{1,0:T(8,128)S(1)} %get-tuple-element.9.query_ref, f32[256,512]{1,0:T(8,128)S(1)} %get-tuple-element.10.skip_ref), custom_call_target="tpu_custom_call" | custom-call | tf_op jit(solution)/shard_map/final/pallas_call | solution.py:316
Async XLA Ops:
  0.0 21.3 %copy-start.2 = (bf16[256,512]{1,0:T(8,128)(2,1)S(1)}, bf16[256,512]{1,0:T(8,128)(2,1)}, u32[]{:S(2)}) copy-start(bf16[256,512]{1,0:T(8,128)(2,1)} %v_ref.1) | copy-start | bytes 786436
  2.3 19.0 %copy-start = (bf16[256,512]{1,0:T(8,128)(2,1)S(1)}, bf16[256,512]{1,0:T(8,128)(2,1)}, u32[]{:S(2)}) copy-start(bf16[256,512]{1,0:T(8,128)(2,1)} %q_ref.1) | copy-start | bytes 786436
  2.3 19.0 %copy-start.1 = (bf16[256,512]{1,0:T(8,128)(2,1)S(1)}, bf16[256,512]{1,0:T(8,128)(2,1)}, u32[]{:S(2)}) copy-start(bf16[256,512]{1,0:T(8,128)(2,1)} %k_ref.1) | copy-start | bytes 786436
  2.3 19.0 %copy-start.3 = (f32[3,256,3]{1,2,0:T(4,128)S(1)}, f32[3,256,3]{1,2,0:T(4,128)}, u32[]{:S(2)}) copy-start(f32[3,256,3]{1,2,0:T(4,128)} %param.10) | copy-start | bytes 27652
  2.4 19.0 %copy-start.5 = (f32[256]{0:T(256)S(1)}, f32[256]{0:T(256)}, u32[]{:S(2)}) copy-start(f32[256]{0:T(256)} %param.13) | copy-start | bytes 3076
  2.4 34.4 %all-to-all-start = ((bf16[32,5,8,128]{3,2,1,0:T(8,128)(2,1)}), bf16[32,5,8,128]{3,2,1,0:T(8,128)(2,1)S(1)}, u32[]{:S(2)}, u32[]{:S(2)}) async-start(bf16[32,5,8,128]{3,2,1,0:T(8,128)(2,1)} %message.1), calls=%async_computation | async-start | bytes 655360 | tf_op jit(solution)/shard_map/all_to_all | solution.py:286
  21.3 0.7 %copy-start.4 = (s32[256]{0:T(256)S(1)}, s32[256]{0:T(256)}, u32[]{:S(2)}) copy-start(s32[256]{0:T(256)} %param.12) | copy-start | bytes 3076

commit v8 on v6

--- a/solution.py
+++ b/solution.py
@@ -76,7 +76,7 @@
     return jnp.dot(columns, pick, preferred_element_type=f32)
 
 
-STORES = 4
+STORES = 8
 
 
 def message_kernel(q_hbm, k_hbm, v_hbm, taps_hbm, filt_hbm, out_hbm, qf, ql, kk, vv, taps_ref, filt_ref, wide_ref, out_ref, sems, out_sems):

time: 67.8 us -> 67.8 us (level)
  no operation moved by 1% of the time
where the time goes in v8:
time: 67.8 us; the launch traced here: 67.5 us
  blocking collectives  26.8 us (40%)
  starting transfers between devices  18.9 us (28%)
  waiting for transfers between devices  13.4 us (20%)
  Pallas kernels  7.55 us (11%)
    all_to_all x1, blocking collectives, shards(): lax.all_to_all(convolved, 'seq', split_axis=0, concat_axis=0, tiled=True,...  26.8 us
    all_to_all x1, starting transfers between devices, shards(): lax.all_to_all(message, 'seq', split_axis=0, concat_axis=0, tiled=True, a...  18.9 us
    all_to_all x1, waiting for transfers between devices, shards(): lax.all_to_all(message, 'seq', split_axis=0, concat_axis=0, tiled=True, a...  13.4 us
    pallas_call x1, Pallas kernels, shards(): pl.pallas_call(conv_kernel, out_shape=jax.ShapeDtypeStruct((PEERS, OWN, B...  3.06 us
    pallas_call x1, Pallas kernels, shards(): pl.pallas_call(message_kernel, out_shape=jax.ShapeDtypeStruct((PEERS, TIL...  2.34 us
    pallas_call x1, Pallas kernels, shards(): pl.pallas_call(gate_kernel, out_shape=[jax.ShapeDtypeStruct((256, BLOCK),...  1.41 us
  transfers between devices with their start and end apart: 1, of which 1 were waited for; matrix products, arithmetic and copies ran while one was open for 0% of the time, Pallas kernels for 2%

profile of v8, /device:TPU:24, one launch (start us, length us, event | category | flops | bytes accessed | tf_op | source)
XLA Modules:
  0.0 67.5 jit_solution(11839031953442531243)
XLA Ops:
  0.0 0.0 copy-start.2
  0.0 2.3 %message.1 = bf16[32,5,8,128]{3,2,1,0:T(8,128)(2,1)} custom-call(bf16[256,512]{1,0:T(8,128)(2,1)} %q_ref.1, bf16[256,512]{1,0:T(8,128)(2,1)} %k_ref.1, bf16[256,512]{1,0:T(8,128)(2,1)} %v_ref.1, f32[3,3,256]{2,1,0:T(4,128)} %bitcast.3, f32[16,512]{1,0:T(8,128)} %filt_hbm.1), custom_call_target="tpu_custom_call" | custom-call | tf_op jit(solution)/shard_map/message/pallas_call | solution.py:265
  2.4 0.0 copy-start
  2.4 0.0 copy-start.1
  2.4 0.0 copy-start.3
  2.4 0.0 copy-start.5
  2.4 18.9 %all-to-all-start = ((bf16[32,5,8,128]{3,2,1,0:T(8,128)(2,1)}), bf16[32,5,8,128]{3,2,1,0:T(8,128)(2,1)S(1)}, u32[]{:S(2)}, u32[]{:S(2)}) async-start(bf16[32,5,8,128]{3,2,1,0:T(8,128)(2,1)} %message.1), calls=%async_computation | async-start | bytes 655360 | tf_op jit(solution)/shard_map/all_to_all | solution.py:284
  21.3 0.0 copy-start.4
  21.3 0.0 copy-done.2
  21.3 0.0 copy-done
  21.3 0.0 copy-done.1
  21.4 0.0 copy-done.3
  21.4 0.0 copy-done.5
  21.4 0.6 copy-done.4
  22.0 1.4 %gate.1 = (f32[256,512]{1,0:T(8,128)S(1)}, f32[256,512]{1,0:T(8,128)S(1)}, f32[5,8,128]{2,1,0:T(8,128)S(1)}) custom-call(bf16[256,512]{1,0:T(8,128)(2,1)S(1)} %copy-done, bf16[256,512]{1,0:T(8,128)(2,1)S(1)} %copy-done.1, bf16[256,512]{1,0:T(8,128)(2,1)S(1)} %copy-done.2, f32[3,3,256]{2,1,0:T(4,128)S(1)} %bitcast.4, s32[1,256]{1,0:T(1,128)S(1)} %bitcast.5, ...), custom_call_target="tpu_custom_call" | custom-call | flops 4000000 | bytes 2097152 | tf_op jit(solution)/shard_map/gate/pallas_call | solution.py:286
  23.4 13.4 %all-to-all-done.msg_ref = bf16[32,5,8,128]{3,2,1,0:T(8,128)(2,1)S(1)} async-done(((bf16[32,5,8,128]{3,2,1,0:T(8,128)(2,1)}), bf16[32,5,8,128]{3,2,1,0:T(8,128)(2,1)S(1)}, u32[]{:S(2)}, u32[]{:S(2)}) %all-to-all-start) | async-done | bytes 327712 | tf_op jit(solution)/shard_map/all_to_all | solution.py:284
  36.8 3.1 %conv.1 = bf16[32,8,512]{2,1,0:T(8,128)(2,1)S(1)} custom-call(bf16[32,5,8,128]{3,2,1,0:T(8,128)(2,1)S(1)} %all-to-all-done.msg_ref, f32[5,8,128]{2,1,0:T(8,128)S(1)} %get-tuple-element.8.aux_ref), custom_call_target="tpu_custom_call" | custom-call | flops 2300000000 | bytes 1048576 | tf_op jit(solution)/shard_map/conv/pallas_call | solution.py:297
  39.9 26.8 %all_to_all.10.back_ref = bf16[32,8,512]{2,1,0:T(8,128)(2,1)S(1)} all-to-all(bf16[32,8,512]{2,1,0:T(8,128)(2,1)S(1)} %conv.1), channel_id=1, replica_groups={{272,0,256,16,32,288,48,304,64,320,80,336,96,352,112,368,128,384,144,40..., dimensions={0} | all-to-all | bytes 524288 | tf_op jit(solution)/shard_map/all_to_all | solution.py:313
  66.7 0.7 %final.1 = bf16[256,512]{1,0:T(8,128)(2,1)} custom-call(bf16[32,8,512]{2,1,0:T(8,128)(2,1)S(1)} %all_to_all.10.back_ref, f32[256,512]{1,0:T(8,128)S(1)} %get-tuple-element.9.query_ref, f32[256,512]{1,0:T(8,128)S(1)} %get-tuple-element.10.skip_ref), custom_call_target="tpu_custom_call" | custom-call | tf_op jit(solution)/shard_map/final/pallas_call | solution.py:314
Async XLA Ops:
  0.0 21.3 %copy-start.2 = (bf16[256,512]{1,0:T(8,128)(2,1)S(1)}, bf16[256,512]{1,0:T(8,128)(2,1)}, u32[]{:S(2)}) copy-start(bf16[256,512]{1,0:T(8,128)(2,1)} %v_ref.1) | copy-start | bytes 786436
  2.4 19.0 %copy-start = (bf16[256,512]{1,0:T(8,128)(2,1)S(1)}, bf16[256,512]{1,0:T(8,128)(2,1)}, u32[]{:S(2)}) copy-start(bf16[256,512]{1,0:T(8,128)(2,1)} %q_ref.1) | copy-start | bytes 786436
  2.4 19.0 %copy-start.1 = (bf16[256,512]{1,0:T(8,128)(2,1)S(1)}, bf16[256,512]{1,0:T(8,128)(2,1)}, u32[]{:S(2)}) copy-start(bf16[256,512]{1,0:T(8,128)(2,1)} %k_ref.1) | copy-start | bytes 786436
  2.4 19.0 %copy-start.3 = (f32[3,256,3]{1,2,0:T(4,128)S(1)}, f32[3,256,3]{1,2,0:T(4,128)}, u32[]{:S(2)}) copy-start(f32[3,256,3]{1,2,0:T(4,128)} %param.10) | copy-start | bytes 27652
  2.4 19.0 %copy-start.5 = (f32[256]{0:T(256)S(1)}, f32[256]{0:T(256)}, u32[]{:S(2)}) copy-start(f32[256]{0:T(256)} %param.13) | copy-start | bytes 3076
  2.4 34.4 %all-to-all-start = ((bf16[32,5,8,128]{3,2,1,0:T(8,128)(2,1)}), bf16[32,5,8,128]{3,2,1,0:T(8,128)(2,1)S(1)}, u32[]{:S(2)}, u32[]{:S(2)}) async-start(bf16[32,5,8,128]{3,2,1,0:T(8,128)(2,1)} %message.1), calls=%async_computation | async-start | bytes 655360 | tf_op jit(solution)/shard_map/all_to_all | solution.py:284
  21.3 0.7 %copy-start.4 = (s32[256]{0:T(256)S(1)}, s32[256]{0:T(256)}, u32[]{:S(2)}) copy-start(s32[256]{0:T(256)} %param.12) | copy-start | bytes 3076

commit v9 on v6

--- a/solution.py
+++ b/solution.py
@@ -316,7 +316,7 @@
         out_shape=jax.ShapeDtypeStruct((256, BLOCK), bf16),
         in_specs=[VMEM] * 3,
         out_specs=HBM,
-        scratch_shapes=[pltpu.VMEM((256, BLOCK), bf16), pltpu.SemaphoreType.DMA((4,))],
+        scratch_shapes=[pltpu.VMEM((256, BLOCK), bf16), pltpu.SemaphoreType.DMA((2,))],
         compiler_params=pltpu.CompilerParams(vmem_limit_bytes=16 << 20),
         name="final",
     )(back, query, skip)

time: 67.8 us -> 67.8 us (level)
  no operation moved by 1% of the time
where the time goes in v9:
time: 67.8 us; the launch traced here: 67.4 us
  blocking collectives  26.8 us (40%)
  starting transfers between devices  18.9 us (28%)
  waiting for transfers between devices  13.4 us (20%)
  Pallas kernels  7.51 us (11%)
    all_to_all x1, blocking collectives, shards(): lax.all_to_all(convolved, 'seq', split_axis=0, concat_axis=0, tiled=True,...  26.8 us
    all_to_all x1, starting transfers between devices, shards(): lax.all_to_all(message, 'seq', split_axis=0, concat_axis=0, tiled=True, a...  18.9 us
    all_to_all x1, waiting for transfers between devices, shards(): lax.all_to_all(message, 'seq', split_axis=0, concat_axis=0, tiled=True, a...  13.4 us
    pallas_call x1, Pallas kernels, shards(): pl.pallas_call(conv_kernel, out_shape=jax.ShapeDtypeStruct((PEERS, OWN, B...  3.06 us
    pallas_call x1, Pallas kernels, shards(): pl.pallas_call(message_kernel, out_shape=jax.ShapeDtypeStruct((PEERS, TIL...  2.3 us
    pallas_call x1, Pallas kernels, shards(): pl.pallas_call(gate_kernel, out_shape=[jax.ShapeDtypeStruct((256, BLOCK),...  1.41 us
  transfers between devices with their start and end apart: 1, of which 1 were waited for; matrix products, arithmetic and copies ran while one was open for 0% of the time, Pallas kernels for 2%

profile of v9, /device:TPU:24, one launch (start us, length us, event | category | flops | bytes accessed | tf_op | source)
XLA Modules:
  0.0 67.4 jit_solution(4424395251647123320)
XLA Ops:
  0.0 0.0 copy-start.2
  0.0 2.3 %message.1 = bf16[32,5,8,128]{3,2,1,0:T(8,128)(2,1)} custom-call(bf16[256,512]{1,0:T(8,128)(2,1)} %q_ref.1, bf16[256,512]{1,0:T(8,128)(2,1)} %k_ref.1, bf16[256,512]{1,0:T(8,128)(2,1)} %v_ref.1, f32[3,3,256]{2,1,0:T(4,128)} %bitcast.3, f32[16,512]{1,0:T(8,128)} %filt_hbm.1), custom_call_target="tpu_custom_call" | custom-call | tf_op jit(solution)/shard_map/message/pallas_call | solution.py:265
  2.3 0.0 copy-start
  2.3 0.0 copy-start.1
  2.3 0.0 copy-start.3
  2.4 0.0 copy-start.5
  2.4 18.9 %all-to-all-start = ((bf16[32,5,8,128]{3,2,1,0:T(8,128)(2,1)}), bf16[32,5,8,128]{3,2,1,0:T(8,128)(2,1)S(1)}, u32[]{:S(2)}, u32[]{:S(2)}) async-start(bf16[32,5,8,128]{3,2,1,0:T(8,128)(2,1)} %message.1), calls=%async_computation | async-start | bytes 655360 | tf_op jit(solution)/shard_map/all_to_all | solution.py:284
  21.3 0.0 copy-start.4
  21.3 0.0 copy-done.2
  21.3 0.0 copy-done
  21.3 0.0 copy-done.1
  21.3 0.0 copy-done.3
  21.3 0.0 copy-done.5
  21.3 0.6 copy-done.4
  22.0 1.4 %gate.1 = (f32[256,512]{1,0:T(8,128)S(1)}, f32[256,512]{1,0:T(8,128)S(1)}, f32[5,8,128]{2,1,0:T(8,128)S(1)}) custom-call(bf16[256,512]{1,0:T(8,128)(2,1)S(1)} %copy-done, bf16[256,512]{1,0:T(8,128)(2,1)S(1)} %copy-done.1, bf16[256,512]{1,0:T(8,128)(2,1)S(1)} %copy-done.2, f32[3,3,256]{2,1,0:T(4,128)S(1)} %bitcast.4, s32[1,256]{1,0:T(1,128)S(1)} %bitcast.5, ...), custom_call_target="tpu_custom_call" | custom-call | flops 4000000 | bytes 2097152 | tf_op jit(solution)/shard_map/gate/pallas_call | solution.py:286
  23.4 13.4 %all-to-all-done.msg_ref = bf16[32,5,8,128]{3,2,1,0:T(8,128)(2,1)S(1)} async-done(((bf16[32,5,8,128]{3,2,1,0:T(8,128)(2,1)}), bf16[32,5,8,128]{3,2,1,0:T(8,128)(2,1)S(1)}, u32[]{:S(2)}, u32[]{:S(2)}) %all-to-all-start) | async-done | bytes 327712 | tf_op jit(solution)/shard_map/all_to_all | solution.py:284
  36.8 3.1 %conv.1 = bf16[32,8,512]{2,1,0:T(8,128)(2,1)S(1)} custom-call(bf16[32,5,8,128]{3,2,1,0:T(8,128)(2,1)S(1)} %all-to-all-done.msg_ref, f32[5,8,128]{2,1,0:T(8,128)S(1)} %get-tuple-element.8.aux_ref), custom_call_target="tpu_custom_call" | custom-call | flops 2300000000 | bytes 1048576 | tf_op jit(solution)/shard_map/conv/pallas_call | solution.py:297
  39.9 26.8 %all_to_all.10.back_ref = bf16[32,8,512]{2,1,0:T(8,128)(2,1)S(1)} all-to-all(bf16[32,8,512]{2,1,0:T(8,128)(2,1)S(1)} %conv.1), channel_id=1, replica_groups={{272,0,256,16,32,288,48,304,64,320,80,336,96,352,112,368,128,384,144,40..., dimensions={0} | all-to-all | bytes 524288 | tf_op jit(solution)/shard_map/all_to_all | solution.py:313
  66.7 0.7 %final.1 = bf16[256,512]{1,0:T(8,128)(2,1)} custom-call(bf16[32,8,512]{2,1,0:T(8,128)(2,1)S(1)} %all_to_all.10.back_ref, f32[256,512]{1,0:T(8,128)S(1)} %get-tuple-element.9.query_ref, f32[256,512]{1,0:T(8,128)S(1)} %get-tuple-element.10.skip_ref), custom_call_target="tpu_custom_call" | custom-call | tf_op jit(solution)/shard_map/final/pallas_call | solution.py:314
Async XLA Ops:
  0.0 21.3 %copy-start.2 = (bf16[256,512]{1,0:T(8,128)(2,1)S(1)}, bf16[256,512]{1,0:T(8,128)(2,1)}, u32[]{:S(2)}) copy-start(bf16[256,512]{1,0:T(8,128)(2,1)} %v_ref.1) | copy-start | bytes 786436
  2.3 19.0 %copy-start = (bf16[256,512]{1,0:T(8,128)(2,1)S(1)}, bf16[256,512]{1,0:T(8,128)(2,1)}, u32[]{:S(2)}) copy-start(bf16[256,512]{1,0:T(8,128)(2,1)} %q_ref.1) | copy-start | bytes 786436
  2.3 19.0 %copy-start.1 = (bf16[256,512]{1,0:T(8,128)(2,1)S(1)}, bf16[256,512]{1,0:T(8,128)(2,1)}, u32[]{:S(2)}) copy-start(bf16[256,512]{1,0:T(8,128)(2,1)} %k_ref.1) | copy-start | bytes 786436
  2.3 19.0 %copy-start.3 = (f32[3,256,3]{1,2,0:T(4,128)S(1)}, f32[3,256,3]{1,2,0:T(4,128)}, u32[]{:S(2)}) copy-start(f32[3,256,3]{1,2,0:T(4,128)} %param.10) | copy-start | bytes 27652
  2.4 19.0 %copy-start.5 = (f32[256]{0:T(256)S(1)}, f32[256]{0:T(256)}, u32[]{:S(2)}) copy-start(f32[256]{0:T(256)} %param.13) | copy-start | bytes 3076
  2.4 34.4 %all-to-all-start = ((bf16[32,5,8,128]{3,2,1,0:T(8,128)(2,1)}), bf16[32,5,8,128]{3,2,1,0:T(8,128)(2,1)S(1)}, u32[]{:S(2)}, u32[]{:S(2)}) async-start(bf16[32,5,8,128]{3,2,1,0:T(8,128)(2,1)} %message.1), calls=%async_computation | async-start | bytes 655360 | tf_op jit(solution)/shard_map/all_to_all | solution.py:284
  21.3 0.7 %copy-start.4 = (s32[256]{0:T(256)S(1)}, s32[256]{0:T(256)}, u32[]{:S(2)}) copy-start(s32[256]{0:T(256)} %param.12) | copy-start | bytes 3076
